TPU v7x, 512 devices: a whole 4x4x16 slice. The times are simulated.
512 devices in a mesh: gx: 16 (over z), gy: 4 (over x_hi, core), gz: 8 (over y, x_lo).
Axes of the slice: x: 4 (x_hi: 2, x_lo: 2; x = x_hi * 2 + x_lo), y: 4, z: 16, core: 2. Of those that a mesh axis runs over, the one named last changes fastest.
Arguments:
- populations_in: float32 [19, 64, 32, 1024], P(None, 'gx', 'gy', 'gz'), as said below
- relax_rates: float32 [15], replicated, may hold values from 0.8 to 1.9
- solid_mask: int32 [64, 32, 1024], P('gx', 'gy', 'gz'), may hold values 0 or 1
- noise_slabs: float32 [4, 3, 32, 1024], P(None, None, 'gy', 'gz'), may hold values from -6 to 6
- half_widths: int32 [3, 2], replicated, may hold values from 2 to 4
Outputs:
- populations: float32 [19, 64, 32, 1024], P(None, 'gx', 'gy', 'gz')
Inputs may be any that keep to these rules, and one draw needn't show every extreme that they name: `solid_mask`: 1 marks a solid node. `populations_in`: each population lies between 0.75 and 1.25 times its lattice weight.
All inputs are finite; a program needn't handle non-finite values. No bound on the sum of `solid_mask` on one device may be relied on, other than what follows from the above.
Results may differ from a plain program's by a relative error of at most 0.0001.
Values sent between devices are 32-bit elements; how exact they have to be, the bound alone decides.
A program may use at most 128 MiB of HBM per device.

v0:
```python
import jax
import jax.numpy as jnp
import numpy as np
from jax import lax
from jax.sharding import PartitionSpec as P

FILT = 8
STEPS = 4


def with_halo(cells, sides, width):
    for axis, dim in sides:
        count = lax.axis_size(axis)
        head = lax.slice_in_dim(cells, 0, width, axis=dim)
        tail = lax.slice_in_dim(cells, cells.shape[dim] - width, cells.shape[dim], axis=dim)
        cells = jnp.concatenate(
            [
                lax.ppermute(tail, axis, [(i, (i + 1) % count) for i in range(count)]),
                cells,
                lax.ppermute(head, axis, [((i + 1) % count, i) for i in range(count)]),
            ],
            axis=dim,
        )
    return cells


def lattice():
    velocity = [
        (0, 0, 0),
        (1, 0, 0),
        (-1, 0, 0),
        (0, 1, 0),
        (0, -1, 0),
        (0, 0, 1),
        (0, 0, -1),
        (1, 1, 0),
        (-1, -1, 0),
        (1, -1, 0),
        (-1, 1, 0),
        (1, 0, 1),
        (-1, 0, -1),
        (1, 0, -1),
        (-1, 0, 1),
        (0, 1, 1),
        (0, -1, -1),
        (0, 1, -1),
        (0, -1, 1),
    ]
    return np.array(velocity) * 1.0


def lattice_weights():
    return np.array([1.0 / 3.0] + [1.0 / 18.0] * 6 + [1.0 / 36.0] * 12)


def opposite():
    return np.array(
        [0] + [number + 1 if number % 2 == 1 else number - 1 for number in range(1, 19)]
    )


def moment_basis():
    speeds = lattice()
    vel_x, vel_y, vel_z = (speeds[:, 0], speeds[:, 1], speeds[:, 2])
    square = vel_x * vel_x + vel_y * vel_y + vel_z * vel_z
    candidates = [
        np.ones(19),
        vel_x,
        vel_y,
        vel_z,
        square,
        vel_x * vel_x - vel_y * vel_y,
        vel_y * vel_y - vel_z * vel_z,
        vel_x * vel_y,
        vel_y * vel_z,
        vel_x * vel_z,
        vel_x * square,
        vel_y * square,
        vel_z * square,
        vel_x * (vel_y * vel_y - vel_z * vel_z),
        vel_y * (vel_z * vel_z - vel_x * vel_x),
        vel_z * (vel_x * vel_x - vel_y * vel_y),
        square * square,
        (vel_x * vel_x - vel_y * vel_y) * square,
        (vel_y * vel_y - vel_z * vel_z) * square,
    ]
    candidates = candidates + list(np.eye(19))
    basis_rows = []
    for vector in candidates:
        remain = np.array(vector) * 1.0
        for earlier in basis_rows:
            remain = remain - np.dot(earlier, remain) * earlier
        length = np.sqrt(np.dot(remain, remain))
        if length > 1e-08 and len(basis_rows) < 19:
            basis_rows.append(remain / length)
    return np.stack(basis_rows)


def collision_kernel(relax_rates):
    moment_rows = jnp.asarray(moment_basis(), jnp.float32)
    relax_full = jnp.concatenate([jnp.zeros((4,), jnp.float32), relax_rates])
    return jnp.einsum(
        "ki,k,kj->ij", moment_rows, relax_full, moment_rows, precision=lax.Precision.HIGHEST
    )


def filter_taps(half_widths):
    offsets = jnp.arange(-FILT, FILT + 1).astype(jnp.float32)
    spread = half_widths.astype(jnp.float32)[..., None]
    weights_yz = jnp.exp(-jnp.pi * offsets * offsets / (2.0 * spread * spread))
    weights_yz = jnp.where(jnp.abs(offsets) <= 2.0 * spread, weights_yz, 0.0)
    return weights_yz / jnp.sqrt(jnp.sum(weights_yz * weights_yz, -1, keepdims=True))


def apply_filter(padded, weights_yz, span_len, height):
    along_span = jnp.zeros(padded.shape[:2] + (span_len, padded.shape[3]), jnp.float32)
    for offset in range(2 * FILT + 1):
        along_span = (
            along_span
            + weights_yz[:, 0, offset][None, :, None, None]
            * padded[:, :, offset : offset + span_len, :]
        )
    result = jnp.zeros(padded.shape[:2] + (span_len, height), jnp.float32)
    for offset in range(2 * FILT + 1):
        result = (
            result
            + weights_yz[:, 1, offset][None, :, None, None]
            * along_span[:, :, :, offset : offset + height]
        )
    return result


def equilibrium(density, vel_field):
    speeds = jnp.asarray(lattice(), jnp.float32)
    weights = jnp.asarray(lattice_weights(), jnp.float32)
    projection = jnp.einsum("qa,a...->q...", speeds, vel_field, precision=lax.Precision.HIGHEST)
    speed_sq = jnp.sum(vel_field * vel_field, 0)
    shape = (19,) + (1,) * density.ndim
    return (
        weights.reshape(shape)
        * density[None]
        * (1.0 + 3.0 * projection + 4.5 * projection * projection - 1.5 * speed_sq[None])
    )


def collide(populations, solid_mask, kernel):
    speeds = jnp.asarray(lattice(), jnp.float32)
    density = jnp.sum(populations, 0)
    momentum = jnp.einsum("qa,q...->a...", speeds, populations, precision=lax.Precision.HIGHEST)
    vel_field = momentum / density[None]
    balance = equilibrium(density, vel_field)
    relaxed = populations - jnp.einsum(
        "ij,j...->i...", kernel, populations - balance, precision=lax.Precision.HIGHEST
    )
    bounced = jnp.stack([populations[int(which)] for which in opposite()])
    return jnp.where(solid_mask[None] > 0, bounced, relaxed)


def inlet_velocity(turbulence_step):
    return jnp.stack(
        [0.05 + 0.05 * turbulence_step[0], 0.05 * turbulence_step[1], 0.05 * turbulence_step[2]]
    )


def local(populations_in, relax_rates, solid_mask, noise_slabs, half_widths):
    kernel = collision_kernel(relax_rates)
    weights_yz = filter_taps(half_widths)
    padded_noise = with_halo(noise_slabs, (("gy", 2), ("gz", 3)), FILT)
    turbulence = apply_filter(padded_noise, weights_yz, noise_slabs.shape[2], noise_slabs.shape[3])
    extent_x, extent_y, extent_z = solid_mask.shape
    speeds = lattice()
    inlet_here = lax.axis_index("gx") == 0
    plane_mask = jnp.logical_and(
        lax.broadcasted_iota(jnp.int32, (1, extent_x, 1, 1), 1) == 0, inlet_here
    )
    populations = populations_in
    for turn in range(STEPS):
        post = collide(populations, solid_mask, kernel)
        padded = with_halo(post, (("gx", 1), ("gy", 2), ("gz", 3)), 1)
        layers = []
        for which in range(19):
            begin_x = 1 - int(speeds[which, 0])
            begin_y = 1 - int(speeds[which, 1])
            begin_z = 1 - int(speeds[which, 2])
            layers.append(
                padded[
                    which,
                    begin_x : begin_x + extent_x,
                    begin_y : begin_y + extent_y,
                    begin_z : begin_z + extent_z,
                ]
            )
        populations = jnp.stack(layers)
        inflow = equilibrium(
            jnp.ones((extent_y, extent_z), jnp.float32), inlet_velocity(turbulence[turn])
        )
        populations = jnp.where(plane_mask, inflow[:, None], populations)
    return populations


def solution(mesh):
    return jax.shard_map(
        local,
        mesh=mesh,
        in_specs=(
            P(None, "gx", "gy", "gz"),
            P(),
            P("gx", "gy", "gz"),
            P(None, None, "gy", "gz"),
            P(),
        ),
        out_specs=P(None, "gx", "gy", "gz"),
        check_vma=False,
    )
```

profile of v0, /device:TPU:1, one launch (start us, length us, event | category | flops | bytes accessed | tf_op | source)
XLA Modules:
  0.0 169.6 jit_solution(12869726806210072225)
XLA Ops:
  0.0 6.2 %collective-permute-start = (f32[4,3,8,128]{3,2,1,0:T(8,128)}, f32[4,3,8,128]{3,2,1,0:T(8,128)S(1)}, u32[]{:S(2)}, u32[]{:S(2)}) collective-permute-start(f32[4,3,8,128]{3,2,1,0:T(8,128)} %param.29), channel_id=1, source_target_pairs={{0,8},{8,16},{16,24},{24,0},{1,9},{9,17},{17,25},{25,1},{2,10},{10... | collective-permute-start | bytes 147464 | tf_op jit(solution)/shard_map/ppermute | solution.py:18
  6.2 4.7 %collective-permute-start.1 = (f32[4,3,8,128]{3,2,1,0:T(8,128)}, f32[4,3,8,128]{3,2,1,0:T(8,128)S(1)}, u32[]{:S(2)}, u32[]{:S(2)}) collective-permute-start(f32[4,3,8,128]{3,2,1,0:T(8,128)} %param.29), channel_id=1, source_target_pairs={{8,0},{16,8},{24,16},{0,24},{9,1},{17,9},{25,17},{1,25},{10,2},{18... | collective-permute-start | bytes 147464 | tf_op jit(solution)/shard_map/ppermute | solution.py:20
  10.8 0.9 fusion.154
  11.9 0.6 copy-done.6
  12.5 0.5 multiply_reduce_fusion.3
  13.1 0.5 fusion.156
  13.6 0.7 copy-done.3
  14.4 0.7 copy-done.7
  15.3 0.5 stack.52
  15.9 0.8 fusion
  16.8 8.4 %collective-permute-start.5 = (f32[19,1,8,128]{3,0,2,1:T(8,128)S(1)}, f32[19,1,8,128]{3,0,2,1:T(8,128)S(1)}, u32[]{:S(2)}, u32[]{:S(2)}) collective-permute-start(f32[19,1,8,128]{3,0,2,1:T(8,128)S(1)} %get-tuple-element.166), channel_id=1, source_target_pairs={{32,0},{64,32},{96,64},{128,96},{160,128},{192,160},{224,192},{256... | collective-permute-start | bytes 233480 | tf_op jit(solution)/shard_map/ppermute | solution.py:20
  25.2 1.9 %collective-permute-start.4 = (f32[19,1,8,128]{3,0,2,1:T(8,128)S(1)}, f32[19,1,8,128]{3,0,2,1:T(8,128)S(1)}, u32[]{:S(2)}, u32[]{:S(2)}) collective-permute-start(f32[19,1,8,128]{3,0,2,1:T(8,128)S(1)} %get-tuple-element.167), channel_id=1, source_target_pairs={{0,32},{32,64},{64,96},{96,128},{128,160},{160,192},{192,224},{224... | collective-permute-start | bytes 233480 | tf_op jit(solution)/shard_map/ppermute | solution.py:18
  27.4 0.8 copy-done.1
  28.3 4.7 %collective-permute-start.3 = (f32[4,3,24,8]{3,2,1,0:T(8,128)S(1)}, f32[4,3,24,8]{3,2,1,0:T(8,128)S(1)}, u32[]{:S(2)}, u32[]{:S(2)}) collective-permute-start(f32[4,3,24,8]{3,2,1,0:T(8,128)S(1)} %get-tuple-element.188), channel_id=1, source_target_pairs={{1,0},{2,1},{3,2},{4,3},{5,4},{6,5},{7,6},{0,7},{9,8},{10,9},{11,1... | collective-permute-start | bytes 27656 | tf_op jit(solution)/shard_map/ppermute | solution.py:20
  33.0 1.9 %collective-permute-start.2 = (f32[4,3,24,8]{3,2,1,0:T(8,128)S(1)}, f32[4,3,24,8]{3,2,1,0:T(8,128)S(1)}, u32[]{:S(2)}, u32[]{:S(2)}) collective-permute-start(f32[4,3,24,8]{3,2,1,0:T(8,128)S(1)} %get-tuple-element.187), channel_id=1, source_target_pairs={{0,1},{1,2},{2,3},{3,4},{4,5},{5,6},{6,7},{7,0},{8,9},{9,10},{10,1... | collective-permute-start | bytes 27656 | tf_op jit(solution)/shard_map/ppermute | solution.py:18
  35.1 5.9 %collective-permute-done.2 = f32[4,3,24,8]{3,2,1,0:T(8,128)S(1)} collective-permute-done((f32[4,3,24,8]{3,2,1,0:T(8,128)S(1)}, f32[4,3,24,8]{3,2,1,0:T(8,128)S(1)}, u32[]{:S(2)}, u32[]{:S(2)}) %collective-permute-start.2) | collective-permute-done | bytes 9248 | tf_op jit(solution)/shard_map/ppermute | solution.py:18
  41.9 0.7 copy-done.8
  42.9 5.1 %collective-permute-start.7 = (f32[19,6,1,128]{3,0,2,1:T(8,128)S(1)}, f32[19,6,1,128]{3,0,2,1:T(8,128)S(1)}, u32[]{:S(2)}, u32[]{:S(2)}) collective-permute-start(f32[19,6,1,128]{3,0,2,1:T(8,128)S(1)} %get-tuple-element.89), channel_id=1, source_target_pairs={{8,0},{16,8},{24,16},{0,24},{9,1},{17,9},{25,17},{1,25},{10,2},{18... | collective-permute-start | bytes 175112 | tf_op jit(solution)/shard_map/ppermute | solution.py:20
  48.0 4.3 %collective-permute-start.6 = (f32[19,6,1,128]{3,0,2,1:T(8,128)S(1)}, f32[19,6,1,128]{3,0,2,1:T(8,128)S(1)}, u32[]{:S(2)}, u32[]{:S(2)}) collective-permute-start(f32[19,6,1,128]{3,0,2,1:T(8,128)S(1)} %get-tuple-element.90), channel_id=1, source_target_pairs={{0,8},{8,16},{16,24},{24,0},{1,9},{9,17},{17,25},{25,1},{2,10},{10... | collective-permute-start | bytes 175112 | tf_op jit(solution)/shard_map/ppermute | solution.py:18
  52.4 1.3 collective-permute-done.6
  54.5 1.9 %collective-permute-start.8 = (f32[19,6,10,1]{0,3,2,1:T(1,128)S(1)}, f32[19,6,10,1]{0,3,2,1:T(1,128)S(1)}, u32[]{:S(2)}, u32[]{:S(2)}) collective-permute-start(f32[19,6,10,1]{0,3,2,1:T(1,128)S(1)} %copy.87), channel_id=1, source_target_pairs={{0,1},{1,2},{2,3},{3,4},{4,5},{5,6},{6,7},{7,0},{8,9},{9,10},{10,1... | collective-permute-start | bytes 13688 | tf_op jit(solution)/shard_map/ppermute | solution.py:18
  56.8 5.5 %collective-permute-start.9 = (f32[19,6,10,1]{0,3,2,1:T(1,128)S(1)}, f32[19,6,10,1]{0,3,2,1:T(1,128)S(1)}, u32[]{:S(2)}, u32[]{:S(2)}) collective-permute-start(f32[19,6,10,1]{0,3,2,1:T(1,128)S(1)} %copy.89), channel_id=1, source_target_pairs={{1,0},{2,1},{3,2},{4,3},{5,4},{6,5},{7,6},{0,7},{9,8},{10,9},{11,1... | collective-permute-start | bytes 13688 | tf_op jit(solution)/shard_map/ppermute | solution.py:20
  62.4 0.5 copy.88
  63.3 0.5 copy.90
  64.3 0.5 stack.53
  65.5 0.5 fusion.157
  66.1 0.5 stack.54
  66.6 0.6 fusion.1
  67.2 4.8 %collective-permute-start.11 = (f32[19,1,8,128]{3,0,2,1:T(8,128)S(1)}, f32[19,1,8,128]{3,0,2,1:T(8,128)S(1)}, u32[]{:S(2)}, u32[]{:S(2)}) collective-permute-start(f32[19,1,8,128]{3,0,2,1:T(8,128)S(1)} %get-tuple-element.144), channel_id=1, source_target_pairs={{32,0},{64,32},{96,64},{128,96},{160,128},{192,160},{224,192},{256... | collective-permute-start | bytes 233480 | tf_op jit(solution)/shard_map/ppermute | solution.py:20
  72.0 1.9 %collective-permute-start.10 = (f32[19,1,8,128]{3,0,2,1:T(8,128)S(1)}, f32[19,1,8,128]{3,0,2,1:T(8,128)S(1)}, u32[]{:S(2)}, u32[]{:S(2)}) collective-permute-start(f32[19,1,8,128]{3,0,2,1:T(8,128)S(1)} %get-tuple-element.145), channel_id=1, source_target_pairs={{0,32},{32,64},{64,96},{96,128},{128,160},{160,192},{192,224},{224... | collective-permute-start | bytes 233480 | tf_op jit(solution)/shard_map/ppermute | solution.py:18
  74.3 4.3 %collective-permute-done.10 = f32[19,1,8,128]{3,0,2,1:T(8,128)S(1)} collective-permute-done((f32[19,1,8,128]{3,0,2,1:T(8,128)S(1)}, f32[19,1,8,128]{3,0,2,1:T(8,128)S(1)}, u32[]{:S(2)}, u32[]{:S(2)}) %collective-permute-start.10) | collective-permute-done | bytes 77856 | tf_op jit(solution)/shard_map/ppermute | solution.py:18
  78.6 6.0 %collective-permute-start.13 = (f32[19,6,1,128]{3,0,2,1:T(8,128)S(1)}, f32[19,6,1,128]{3,0,2,1:T(8,128)S(1)}, u32[]{:S(2)}, u32[]{:S(2)}) collective-permute-start(f32[19,6,1,128]{3,0,2,1:T(8,128)S(1)} %get-tuple-element.86), channel_id=1, source_target_pairs={{8,0},{16,8},{24,16},{0,24},{9,1},{17,9},{25,17},{1,25},{10,2},{18... | collective-permute-start | bytes 175112 | tf_op jit(solution)/shard_map/ppermute | solution.py:20
  84.7 4.2 %collective-permute-start.12 = (f32[19,6,1,128]{3,0,2,1:T(8,128)S(1)}, f32[19,6,1,128]{3,0,2,1:T(8,128)S(1)}, u32[]{:S(2)}, u32[]{:S(2)}) collective-permute-start(f32[19,6,1,128]{3,0,2,1:T(8,128)S(1)} %get-tuple-element.87), channel_id=1, source_target_pairs={{0,8},{8,16},{16,24},{24,0},{1,9},{9,17},{17,25},{25,1},{2,10},{10... | collective-permute-start | bytes 175112 | tf_op jit(solution)/shard_map/ppermute | solution.py:18
  89.0 1.3 collective-permute-done.12
  91.1 1.9 %collective-permute-start.14 = (f32[19,6,10,1]{0,3,2,1:T(1,128)S(1)}, f32[19,6,10,1]{0,3,2,1:T(1,128)S(1)}, u32[]{:S(2)}, u32[]{:S(2)}) collective-permute-start(f32[19,6,10,1]{0,3,2,1:T(1,128)S(1)} %copy.92), channel_id=1, source_target_pairs={{0,1},{1,2},{2,3},{3,4},{4,5},{5,6},{6,7},{7,0},{8,9},{9,10},{10,1... | collective-permute-start | bytes 13688 | tf_op jit(solution)/shard_map/ppermute | solution.py:18
  93.4 5.6 %collective-permute-start.15 = (f32[19,6,10,1]{0,3,2,1:T(1,128)S(1)}, f32[19,6,10,1]{0,3,2,1:T(1,128)S(1)}, u32[]{:S(2)}, u32[]{:S(2)}) collective-permute-start(f32[19,6,10,1]{0,3,2,1:T(1,128)S(1)} %copy.94), channel_id=1, source_target_pairs={{1,0},{2,1},{3,2},{4,3},{5,4},{6,5},{7,6},{0,7},{9,8},{10,9},{11,1... | collective-permute-start | bytes 13688 | tf_op jit(solution)/shard_map/ppermute | solution.py:20
  99.2 0.5 copy.93
  100.0 0.5 copy.95
  100.9 0.5 stack.55
  102.2 0.5 fusion.158
  103.3 0.6 fusion.2
  103.9 1.9 %collective-permute-start.17 = (f32[19,1,8,128]{3,0,2,1:T(8,128)S(1)}, f32[19,1,8,128]{3,0,2,1:T(8,128)S(1)}, u32[]{:S(2)}, u32[]{:S(2)}) collective-permute-start(f32[19,1,8,128]{3,0,2,1:T(8,128)S(1)} %get-tuple-element.122), channel_id=1, source_target_pairs={{32,0},{64,32},{96,64},{128,96},{160,128},{192,160},{224,192},{256... | collective-permute-start | bytes 233480 | tf_op jit(solution)/shard_map/ppermute | solution.py:20
  105.8 3.4 %collective-permute-start.16 = (f32[19,1,8,128]{3,0,2,1:T(8,128)S(1)}, f32[19,1,8,128]{3,0,2,1:T(8,128)S(1)}, u32[]{:S(2)}, u32[]{:S(2)}) collective-permute-start(f32[19,1,8,128]{3,0,2,1:T(8,128)S(1)} %get-tuple-element.123), channel_id=1, source_target_pairs={{0,32},{32,64},{64,96},{96,128},{128,160},{160,192},{192,224},{224... | collective-permute-start | bytes 233480 | tf_op jit(solution)/shard_map/ppermute | solution.py:18
  109.2 3.1 %collective-permute-done.16 = f32[19,1,8,128]{3,0,2,1:T(8,128)S(1)} collective-permute-done((f32[19,1,8,128]{3,0,2,1:T(8,128)S(1)}, f32[19,1,8,128]{3,0,2,1:T(8,128)S(1)}, u32[]{:S(2)}, u32[]{:S(2)}) %collective-permute-start.16) | collective-permute-done | bytes 77856 | tf_op jit(solution)/shard_map/ppermute | solution.py:18
  112.4 6.0 %collective-permute-start.19 = (f32[19,6,1,128]{3,0,2,1:T(8,128)S(1)}, f32[19,6,1,128]{3,0,2,1:T(8,128)S(1)}, u32[]{:S(2)}, u32[]{:S(2)}) collective-permute-start(f32[19,6,1,128]{3,0,2,1:T(8,128)S(1)} %get-tuple-element.83), channel_id=1, source_target_pairs={{8,0},{16,8},{24,16},{0,24},{9,1},{17,9},{25,17},{1,25},{10,2},{18... | collective-permute-start | bytes 175112 | tf_op jit(solution)/shard_map/ppermute | solution.py:20
  118.3 4.2 %collective-permute-start.18 = (f32[19,6,1,128]{3,0,2,1:T(8,128)S(1)}, f32[19,6,1,128]{3,0,2,1:T(8,128)S(1)}, u32[]{:S(2)}, u32[]{:S(2)}) collective-permute-start(f32[19,6,1,128]{3,0,2,1:T(8,128)S(1)} %get-tuple-element.84), channel_id=1, source_target_pairs={{0,8},{8,16},{16,24},{24,0},{1,9},{9,17},{17,25},{25,1},{2,10},{10... | collective-permute-start | bytes 175112 | tf_op jit(solution)/shard_map/ppermute | solution.py:18
  123.0 1.0 collective-permute-done.18
  124.8 1.9 %collective-permute-start.20 = (f32[19,6,10,1]{0,3,2,1:T(1,128)S(1)}, f32[19,6,10,1]{0,3,2,1:T(1,128)S(1)}, u32[]{:S(2)}, u32[]{:S(2)}) collective-permute-start(f32[19,6,10,1]{0,3,2,1:T(1,128)S(1)} %copy.97), channel_id=1, source_target_pairs={{0,1},{1,2},{2,3},{3,4},{4,5},{5,6},{6,7},{7,0},{8,9},{9,10},{10,1... | collective-permute-start | bytes 13688 | tf_op jit(solution)/shard_map/ppermute | solution.py:18
  127.1 5.5 %collective-permute-start.21 = (f32[19,6,10,1]{0,3,2,1:T(1,128)S(1)}, f32[19,6,10,1]{0,3,2,1:T(1,128)S(1)}, u32[]{:S(2)}, u32[]{:S(2)}) collective-permute-start(f32[19,6,10,1]{0,3,2,1:T(1,128)S(1)} %copy.99), channel_id=1, source_target_pairs={{1,0},{2,1},{3,2},{4,3},{5,4},{6,5},{7,6},{0,7},{9,8},{10,9},{11,1... | collective-permute-start | bytes 13688 | tf_op jit(solution)/shard_map/ppermute | solution.py:20
  132.7 0.5 copy.98
  133.6 0.5 copy.100
  135.8 0.5 fusion.159
  136.9 0.6 fusion.3
  137.5 1.9 %collective-permute-start.23 = (f32[19,1,8,128]{3,0,2,1:T(8,128)S(1)}, f32[19,1,8,128]{3,0,2,1:T(8,128)S(1)}, u32[]{:S(2)}, u32[]{:S(2)}) collective-permute-start(f32[19,1,8,128]{3,0,2,1:T(8,128)S(1)} %get-tuple-element.100), channel_id=1, source_target_pairs={{32,0},{64,32},{96,64},{128,96},{160,128},{192,160},{224,192},{256... | collective-permute-start | bytes 233480 | tf_op jit(solution)/shard_map/ppermute | solution.py:20
  139.4 3.4 %collective-permute-start.22 = (f32[19,1,8,128]{3,0,2,1:T(8,128)S(1)}, f32[19,1,8,128]{3,0,2,1:T(8,128)S(1)}, u32[]{:S(2)}, u32[]{:S(2)}) collective-permute-start(f32[19,1,8,128]{3,0,2,1:T(8,128)S(1)} %get-tuple-element.101), channel_id=1, source_target_pairs={{0,32},{32,64},{64,96},{96,128},{128,160},{160,192},{192,224},{224... | collective-permute-start | bytes 233480 | tf_op jit(solution)/shard_map/ppermute | solution.py:18
  142.8 3.1 %collective-permute-done.22 = f32[19,1,8,128]{3,0,2,1:T(8,128)S(1)} collective-permute-done((f32[19,1,8,128]{3,0,2,1:T(8,128)S(1)}, f32[19,1,8,128]{3,0,2,1:T(8,128)S(1)}, u32[]{:S(2)}, u32[]{:S(2)}) %collective-permute-start.22) | collective-permute-done | bytes 77856 | tf_op jit(solution)/shard_map/ppermute | solution.py:18
  146.0 6.0 %collective-permute-start.25 = (f32[19,6,1,128]{3,0,2,1:T(8,128)S(1)}, f32[19,6,1,128]{3,0,2,1:T(8,128)S(1)}, u32[]{:S(2)}, u32[]{:S(2)}) collective-permute-start(f32[19,6,1,128]{3,0,2,1:T(8,128)S(1)} %get-tuple-element.80), channel_id=1, source_target_pairs={{8,0},{16,8},{24,16},{0,24},{9,1},{17,9},{25,17},{1,25},{10,2},{18... | collective-permute-start | bytes 175112 | tf_op jit(solution)/shard_map/ppermute | solution.py:20
  152.1 4.2 %collective-permute-start.24 = (f32[19,6,1,128]{3,0,2,1:T(8,128)S(1)}, f32[19,6,1,128]{3,0,2,1:T(8,128)S(1)}, u32[]{:S(2)}, u32[]{:S(2)}) collective-permute-start(f32[19,6,1,128]{3,0,2,1:T(8,128)S(1)} %get-tuple-element.81), channel_id=1, source_target_pairs={{0,8},{8,16},{16,24},{24,0},{1,9},{9,17},{17,25},{25,1},{2,10},{10... | collective-permute-start | bytes 175112 | tf_op jit(solution)/shard_map/ppermute | solution.py:18
  156.6 1.1 collective-permute-done.24
  158.4 1.9 %collective-permute-start.26 = (f32[19,6,10,1]{0,3,2,1:T(1,128)S(1)}, f32[19,6,10,1]{0,3,2,1:T(1,128)S(1)}, u32[]{:S(2)}, u32[]{:S(2)}) collective-permute-start(f32[19,6,10,1]{0,3,2,1:T(1,128)S(1)} %copy.102), channel_id=1, source_target_pairs={{0,1},{1,2},{2,3},{3,4},{4,5},{5,6},{6,7},{7,0},{8,9},{9,10},{10,1... | collective-permute-start | bytes 13688 | tf_op jit(solution)/shard_map/ppermute | solution.py:18
  160.8 5.5 %collective-permute-start.27 = (f32[19,6,10,1]{0,3,2,1:T(1,128)S(1)}, f32[19,6,10,1]{0,3,2,1:T(1,128)S(1)}, u32[]{:S(2)}, u32[]{:S(2)}) collective-permute-start(f32[19,6,10,1]{0,3,2,1:T(1,128)S(1)} %copy.104), channel_id=1, source_target_pairs={{1,0},{2,1},{3,2},{4,3},{5,4},{6,5},{7,6},{0,7},{9,8},{10,9},{11,1... | collective-permute-start | bytes 13688 | tf_op jit(solution)/shard_map/ppermute | solution.py:20
  166.4 0.5 copy.103
  167.3 0.5 copy.105
  168.8 0.8 copy.106
  (127 shorter events, 16.4 us)
Async XLA Ops:
  0.0 11.8 %copy-start = (f32[19,4,8,128]{3,2,1,0:T(8,128)S(1)}, f32[19,4,8,128]{3,2,1,0:T(8,128)}, u32[]{:S(2)}) copy-start(f32[19,4,8,128]{3,2,1,0:T(8,128)} %param.26) | copy-start | bytes 933892
  0.0 27.4 %collective-permute-start = (f32[4,3,8,128]{3,2,1,0:T(8,128)}, f32[4,3,8,128]{3,2,1,0:T(8,128)S(1)}, u32[]{:S(2)}, u32[]{:S(2)}) collective-permute-start(f32[4,3,8,128]{3,2,1,0:T(8,128)} %param.29), channel_id=1, source_target_pairs={{0,8},{8,16},{16,24},{24,0},{1,9},{9,17},{17,25},{25,1},{2,10},{10... | collective-permute-start | bytes 147464 | tf_op jit(solution)/shard_map/ppermute | solution.py:18
  6.2 22.0 %collective-permute-start.1 = (f32[4,3,8,128]{3,2,1,0:T(8,128)}, f32[4,3,8,128]{3,2,1,0:T(8,128)S(1)}, u32[]{:S(2)}, u32[]{:S(2)}) collective-permute-start(f32[4,3,8,128]{3,2,1,0:T(8,128)} %param.29), channel_id=1, source_target_pairs={{8,0},{16,8},{24,16},{0,24},{9,1},{17,9},{25,17},{1,25},{10,2},{18... | collective-permute-start | bytes 147464 | tf_op jit(solution)/shard_map/ppermute | solution.py:20
  11.8 0.7 copy-start.6
  11.8 0.7 copy-start.2
  13.6 0.7 copy-start.3
  14.3 0.7 copy-start.7
  15.3 0.7 copy-start.4
  16.8 26.1 %collective-permute-start.5 = (f32[19,1,8,128]{3,0,2,1:T(8,128)S(1)}, f32[19,1,8,128]{3,0,2,1:T(8,128)S(1)}, u32[]{:S(2)}, u32[]{:S(2)}) collective-permute-start(f32[19,1,8,128]{3,0,2,1:T(8,128)S(1)} %get-tuple-element.166), channel_id=1, source_target_pairs={{32,0},{64,32},{96,64},{128,96},{160,128},{192,160},{224,192},{256... | collective-permute-start | bytes 233480 | tf_op jit(solution)/shard_map/ppermute | solution.py:20
  25.2 2.0 %copy-start.5 = (s32[3,2]{0,1:T(2,128)S(1)}, s32[3,2]{0,1:T(2,128)}, u32[]{:S(2)}) copy-start(s32[3,2]{0,1:T(2,128)} %param.30) | copy-start | bytes 76
  25.2 17.7 %collective-permute-start.4 = (f32[19,1,8,128]{3,0,2,1:T(8,128)S(1)}, f32[19,1,8,128]{3,0,2,1:T(8,128)S(1)}, u32[]{:S(2)}, u32[]{:S(2)}) collective-permute-start(f32[19,1,8,128]{3,0,2,1:T(8,128)S(1)} %get-tuple-element.167), channel_id=1, source_target_pairs={{0,32},{32,64},{64,96},{96,128},{128,160},{160,192},{192,224},{224... | collective-permute-start | bytes 233480 | tf_op jit(solution)/shard_map/ppermute | solution.py:18
  27.4 0.8 copy-start.1
  28.3 6.8 %collective-permute-start.3 = (f32[4,3,24,8]{3,2,1,0:T(8,128)S(1)}, f32[4,3,24,8]{3,2,1,0:T(8,128)S(1)}, u32[]{:S(2)}, u32[]{:S(2)}) collective-permute-start(f32[4,3,24,8]{3,2,1,0:T(8,128)S(1)} %get-tuple-element.188), channel_id=1, source_target_pairs={{1,0},{2,1},{3,2},{4,3},{5,4},{6,5},{7,6},{0,7},{9,8},{10,9},{11,1... | collective-permute-start | bytes 27656 | tf_op jit(solution)/shard_map/ppermute | solution.py:20
  33.0 8.0 %collective-permute-start.2 = (f32[4,3,24,8]{3,2,1,0:T(8,128)S(1)}, f32[4,3,24,8]{3,2,1,0:T(8,128)S(1)}, u32[]{:S(2)}, u32[]{:S(2)}) collective-permute-start(f32[4,3,24,8]{3,2,1,0:T(8,128)S(1)} %get-tuple-element.187), channel_id=1, source_target_pairs={{0,1},{1,2},{2,3},{3,4},{4,5},{5,6},{6,7},{7,0},{8,9},{9,10},{10,1... | collective-permute-start | bytes 27656 | tf_op jit(solution)/shard_map/ppermute | solution.py:18
  41.8 0.7 copy-start.8
  42.9 9.5 %collective-permute-start.7 = (f32[19,6,1,128]{3,0,2,1:T(8,128)S(1)}, f32[19,6,1,128]{3,0,2,1:T(8,128)S(1)}, u32[]{:S(2)}, u32[]{:S(2)}) collective-permute-start(f32[19,6,1,128]{3,0,2,1:T(8,128)S(1)} %get-tuple-element.89), channel_id=1, source_target_pairs={{8,0},{16,8},{24,16},{0,24},{9,1},{17,9},{25,17},{1,25},{10,2},{18... | collective-permute-start | bytes 175112 | tf_op jit(solution)/shard_map/ppermute | solution.py:20
  48.0 5.6 %collective-permute-start.6 = (f32[19,6,1,128]{3,0,2,1:T(8,128)S(1)}, f32[19,6,1,128]{3,0,2,1:T(8,128)S(1)}, u32[]{:S(2)}, u32[]{:S(2)}) collective-permute-start(f32[19,6,1,128]{3,0,2,1:T(8,128)S(1)} %get-tuple-element.90), channel_id=1, source_target_pairs={{0,8},{8,16},{16,24},{24,0},{1,9},{9,17},{17,25},{25,1},{2,10},{10... | collective-permute-start | bytes 175112 | tf_op jit(solution)/shard_map/ppermute | solution.py:18
  54.5 7.9 %collective-permute-start.8 = (f32[19,6,10,1]{0,3,2,1:T(1,128)S(1)}, f32[19,6,10,1]{0,3,2,1:T(1,128)S(1)}, u32[]{:S(2)}, u32[]{:S(2)}) collective-permute-start(f32[19,6,10,1]{0,3,2,1:T(1,128)S(1)} %copy.87), channel_id=1, source_target_pairs={{0,1},{1,2},{2,3},{3,4},{4,5},{5,6},{6,7},{7,0},{8,9},{9,10},{10,1... | collective-permute-start | bytes 13688 | tf_op jit(solution)/shard_map/ppermute | solution.py:18
  56.8 6.5 %collective-permute-start.9 = (f32[19,6,10,1]{0,3,2,1:T(1,128)S(1)}, f32[19,6,10,1]{0,3,2,1:T(1,128)S(1)}, u32[]{:S(2)}, u32[]{:S(2)}) collective-permute-start(f32[19,6,10,1]{0,3,2,1:T(1,128)S(1)} %copy.89), channel_id=1, source_target_pairs={{1,0},{2,1},{3,2},{4,3},{5,4},{6,5},{7,6},{0,7},{9,8},{10,9},{11,1... | collective-permute-start | bytes 13688 | tf_op jit(solution)/shard_map/ppermute | solution.py:20
  67.2 7.1 %collective-permute-start.11 = (f32[19,1,8,128]{3,0,2,1:T(8,128)S(1)}, f32[19,1,8,128]{3,0,2,1:T(8,128)S(1)}, u32[]{:S(2)}, u32[]{:S(2)}) collective-permute-start(f32[19,1,8,128]{3,0,2,1:T(8,128)S(1)} %get-tuple-element.144), channel_id=1, source_target_pairs={{32,0},{64,32},{96,64},{128,96},{160,128},{192,160},{224,192},{256... | collective-permute-start | bytes 233480 | tf_op jit(solution)/shard_map/ppermute | solution.py:20
  72.0 6.6 %collective-permute-start.10 = (f32[19,1,8,128]{3,0,2,1:T(8,128)S(1)}, f32[19,1,8,128]{3,0,2,1:T(8,128)S(1)}, u32[]{:S(2)}, u32[]{:S(2)}) collective-permute-start(f32[19,1,8,128]{3,0,2,1:T(8,128)S(1)} %get-tuple-element.145), channel_id=1, source_target_pairs={{0,32},{32,64},{64,96},{96,128},{128,160},{160,192},{192,224},{224... | collective-permute-start | bytes 233480 | tf_op jit(solution)/shard_map/ppermute | solution.py:18
  78.6 10.4 %collective-permute-start.13 = (f32[19,6,1,128]{3,0,2,1:T(8,128)S(1)}, f32[19,6,1,128]{3,0,2,1:T(8,128)S(1)}, u32[]{:S(2)}, u32[]{:S(2)}) collective-permute-start(f32[19,6,1,128]{3,0,2,1:T(8,128)S(1)} %get-tuple-element.86), channel_id=1, source_target_pairs={{8,0},{16,8},{24,16},{0,24},{9,1},{17,9},{25,17},{1,25},{10,2},{18... | collective-permute-start | bytes 175112 | tf_op jit(solution)/shard_map/ppermute | solution.py:20
  84.7 5.6 %collective-permute-start.12 = (f32[19,6,1,128]{3,0,2,1:T(8,128)S(1)}, f32[19,6,1,128]{3,0,2,1:T(8,128)S(1)}, u32[]{:S(2)}, u32[]{:S(2)}) collective-permute-start(f32[19,6,1,128]{3,0,2,1:T(8,128)S(1)} %get-tuple-element.87), channel_id=1, source_target_pairs={{0,8},{8,16},{16,24},{24,0},{1,9},{9,17},{17,25},{25,1},{2,10},{10... | collective-permute-start | bytes 175112 | tf_op jit(solution)/shard_map/ppermute | solution.py:18
  91.1 8.1 %collective-permute-start.14 = (f32[19,6,10,1]{0,3,2,1:T(1,128)S(1)}, f32[19,6,10,1]{0,3,2,1:T(1,128)S(1)}, u32[]{:S(2)}, u32[]{:S(2)}) collective-permute-start(f32[19,6,10,1]{0,3,2,1:T(1,128)S(1)} %copy.92), channel_id=1, source_target_pairs={{0,1},{1,2},{2,3},{3,4},{4,5},{5,6},{6,7},{7,0},{8,9},{9,10},{10,1... | collective-permute-start | bytes 13688 | tf_op jit(solution)/shard_map/ppermute | solution.py:18
  93.4 6.5 %collective-permute-start.15 = (f32[19,6,10,1]{0,3,2,1:T(1,128)S(1)}, f32[19,6,10,1]{0,3,2,1:T(1,128)S(1)}, u32[]{:S(2)}, u32[]{:S(2)}) collective-permute-start(f32[19,6,10,1]{0,3,2,1:T(1,128)S(1)} %copy.94), channel_id=1, source_target_pairs={{1,0},{2,1},{3,2},{4,3},{5,4},{6,5},{7,6},{0,7},{9,8},{10,9},{11,1... | collective-permute-start | bytes 13688 | tf_op jit(solution)/shard_map/ppermute | solution.py:20
  103.9 5.4 %collective-permute-start.17 = (f32[19,1,8,128]{3,0,2,1:T(8,128)S(1)}, f32[19,1,8,128]{3,0,2,1:T(8,128)S(1)}, u32[]{:S(2)}, u32[]{:S(2)}) collective-permute-start(f32[19,1,8,128]{3,0,2,1:T(8,128)S(1)} %get-tuple-element.122), channel_id=1, source_target_pairs={{32,0},{64,32},{96,64},{128,96},{160,128},{192,160},{224,192},{256... | collective-permute-start | bytes 233480 | tf_op jit(solution)/shard_map/ppermute | solution.py:20
  105.8 6.6 %collective-permute-start.16 = (f32[19,1,8,128]{3,0,2,1:T(8,128)S(1)}, f32[19,1,8,128]{3,0,2,1:T(8,128)S(1)}, u32[]{:S(2)}, u32[]{:S(2)}) collective-permute-start(f32[19,1,8,128]{3,0,2,1:T(8,128)S(1)} %get-tuple-element.123), channel_id=1, source_target_pairs={{0,32},{32,64},{64,96},{96,128},{128,160},{160,192},{192,224},{224... | collective-permute-start | bytes 233480 | tf_op jit(solution)/shard_map/ppermute | solution.py:18
  112.4 10.6 %collective-permute-start.19 = (f32[19,6,1,128]{3,0,2,1:T(8,128)S(1)}, f32[19,6,1,128]{3,0,2,1:T(8,128)S(1)}, u32[]{:S(2)}, u32[]{:S(2)}) collective-permute-start(f32[19,6,1,128]{3,0,2,1:T(8,128)S(1)} %get-tuple-element.83), channel_id=1, source_target_pairs={{8,0},{16,8},{24,16},{0,24},{9,1},{17,9},{25,17},{1,25},{10,2},{18... | collective-permute-start | bytes 175112 | tf_op jit(solution)/shard_map/ppermute | solution.py:20
  118.3 5.6 %collective-permute-start.18 = (f32[19,6,1,128]{3,0,2,1:T(8,128)S(1)}, f32[19,6,1,128]{3,0,2,1:T(8,128)S(1)}, u32[]{:S(2)}, u32[]{:S(2)}) collective-permute-start(f32[19,6,1,128]{3,0,2,1:T(8,128)S(1)} %get-tuple-element.84), channel_id=1, source_target_pairs={{0,8},{8,16},{16,24},{24,0},{1,9},{9,17},{17,25},{25,1},{2,10},{10... | collective-permute-start | bytes 175112 | tf_op jit(solution)/shard_map/ppermute | solution.py:18
  124.8 7.9 %collective-permute-start.20 = (f32[19,6,10,1]{0,3,2,1:T(1,128)S(1)}, f32[19,6,10,1]{0,3,2,1:T(1,128)S(1)}, u32[]{:S(2)}, u32[]{:S(2)}) collective-permute-start(f32[19,6,10,1]{0,3,2,1:T(1,128)S(1)} %copy.97), channel_id=1, source_target_pairs={{0,1},{1,2},{2,3},{3,4},{4,5},{5,6},{6,7},{7,0},{8,9},{9,10},{10,1... | collective-permute-start | bytes 13688 | tf_op jit(solution)/shard_map/ppermute | solution.py:18
  127.1 6.5 %collective-permute-start.21 = (f32[19,6,10,1]{0,3,2,1:T(1,128)S(1)}, f32[19,6,10,1]{0,3,2,1:T(1,128)S(1)}, u32[]{:S(2)}, u32[]{:S(2)}) collective-permute-start(f32[19,6,10,1]{0,3,2,1:T(1,128)S(1)} %copy.99), channel_id=1, source_target_pairs={{1,0},{2,1},{3,2},{4,3},{5,4},{6,5},{7,6},{0,7},{9,8},{10,9},{11,1... | collective-permute-start | bytes 13688 | tf_op jit(solution)/shard_map/ppermute | solution.py:20
  137.5 5.4 %collective-permute-start.23 = (f32[19,1,8,128]{3,0,2,1:T(8,128)S(1)}, f32[19,1,8,128]{3,0,2,1:T(8,128)S(1)}, u32[]{:S(2)}, u32[]{:S(2)}) collective-permute-start(f32[19,1,8,128]{3,0,2,1:T(8,128)S(1)} %get-tuple-element.100), channel_id=1, source_target_pairs={{32,0},{64,32},{96,64},{128,96},{160,128},{192,160},{224,192},{256... | collective-permute-start | bytes 233480 | tf_op jit(solution)/shard_map/ppermute | solution.py:20
  139.4 6.6 %collective-permute-start.22 = (f32[19,1,8,128]{3,0,2,1:T(8,128)S(1)}, f32[19,1,8,128]{3,0,2,1:T(8,128)S(1)}, u32[]{:S(2)}, u32[]{:S(2)}) collective-permute-start(f32[19,1,8,128]{3,0,2,1:T(8,128)S(1)} %get-tuple-element.101), channel_id=1, source_target_pairs={{0,32},{32,64},{64,96},{96,128},{128,160},{160,192},{192,224},{224... | collective-permute-start | bytes 233480 | tf_op jit(solution)/shard_map/ppermute | solution.py:18
  146.0 10.6 %collective-permute-start.25 = (f32[19,6,1,128]{3,0,2,1:T(8,128)S(1)}, f32[19,6,1,128]{3,0,2,1:T(8,128)S(1)}, u32[]{:S(2)}, u32[]{:S(2)}) collective-permute-start(f32[19,6,1,128]{3,0,2,1:T(8,128)S(1)} %get-tuple-element.80), channel_id=1, source_target_pairs={{8,0},{16,8},{24,16},{0,24},{9,1},{17,9},{25,17},{1,25},{10,2},{18... | collective-permute-start | bytes 175112 | tf_op jit(solution)/shard_map/ppermute | solution.py:20
  152.1 5.6 %collective-permute-start.24 = (f32[19,6,1,128]{3,0,2,1:T(8,128)S(1)}, f32[19,6,1,128]{3,0,2,1:T(8,128)S(1)}, u32[]{:S(2)}, u32[]{:S(2)}) collective-permute-start(f32[19,6,1,128]{3,0,2,1:T(8,128)S(1)} %get-tuple-element.81), channel_id=1, source_target_pairs={{0,8},{8,16},{16,24},{24,0},{1,9},{9,17},{17,25},{25,1},{2,10},{10... | collective-permute-start | bytes 175112 | tf_op jit(solution)/shard_map/ppermute | solution.py:18
  158.4 7.9 %collective-permute-start.26 = (f32[19,6,10,1]{0,3,2,1:T(1,128)S(1)}, f32[19,6,10,1]{0,3,2,1:T(1,128)S(1)}, u32[]{:S(2)}, u32[]{:S(2)}) collective-permute-start(f32[19,6,10,1]{0,3,2,1:T(1,128)S(1)} %copy.102), channel_id=1, source_target_pairs={{0,1},{1,2},{2,3},{3,4},{4,5},{5,6},{6,7},{7,0},{8,9},{9,10},{10,1... | collective-permute-start | bytes 13688 | tf_op jit(solution)/shard_map/ppermute | solution.py:18
  160.8 6.5 %collective-permute-start.27 = (f32[19,6,10,1]{0,3,2,1:T(1,128)S(1)}, f32[19,6,10,1]{0,3,2,1:T(1,128)S(1)}, u32[]{:S(2)}, u32[]{:S(2)}) collective-permute-start(f32[19,6,10,1]{0,3,2,1:T(1,128)S(1)} %copy.104), channel_id=1, source_target_pairs={{1,0},{2,1},{3,2},{4,3},{5,4},{6,5},{7,6},{0,7},{9,8},{10,9},{11,1... | collective-permute-start | bytes 13688 | tf_op jit(solution)/shard_map/ppermute | solution.py:20
where the time goes:
time: 173 us; the launch traced here: 170 us
  starting transfers between devices  115 us (66%)
  waiting for transfers between devices  21.9 us (13%)
  local copies, waits for them, and re-layouts  18.8 us (11%)
  matrix products  7.83 us (5%)
  other arithmetic  5.21 us (3%)
    ppermute x14, starting transfers between devices, with_halo(): lax.ppermute(head, axis, [((i + 1) % count, i) for i in range(count)])  71.6 us
    ppermute x14, starting transfers between devices, with_halo(): lax.ppermute(tail, axis, [(i, (i + 1) % count) for i in range(count)])  43.3 us
    ppermute x14, waiting for transfers between devices, with_halo(): lax.ppermute(tail, axis, [(i, (i + 1) % count) for i in range(count)])  21.2 us
    unnamed x20, local copies, waits for them, and re-layouts  3.65 us
    dot_general x8, matrix products, equilibrium(): jnp.einsum('qa,a...->q...', speeds, vel_field, precision=lax.Precision.HI...  3.46 us
  transfers between devices with their start and end apart: 28, of which 16 were waited for; matrix products, arithmetic and copies ran while one was open for 7% of the time, Pallas kernels for 0%

commit v1 on v0

v1 whole, which is shorter than its diff:
```python
import functools
import itertools

import jax
import jax.numpy as jnp
from jax import lax
from jax.experimental import pallas as pl
from jax.experimental.pallas import tpu as pltpu
from jax.sharding import PartitionSpec as P

MESH = pl.DeviceIdType.MESH
AXES = ("gx", "gy", "gz")
FILT = 8
STEPS = 4
NX, NY, NZ = 4, 8, 128
VELOCITY = [
    (0, 0, 0),
    (1, 0, 0),
    (-1, 0, 0),
    (0, 1, 0),
    (0, -1, 0),
    (0, 0, 1),
    (0, 0, -1),
    (1, 1, 0),
    (-1, -1, 0),
    (1, -1, 0),
    (-1, 1, 0),
    (1, 0, 1),
    (-1, 0, -1),
    (1, 0, -1),
    (-1, 0, 1),
    (0, 1, 1),
    (0, -1, -1),
    (0, 1, -1),
    (0, -1, 1),
]
OPPOSITE = [0] + [q + 1 if q % 2 == 1 else q - 1 for q in range(1, 19)]
ORDER = sorted(range(19), key=lambda q: -VELOCITY[q][0])
PLACE = [ORDER.index(q) for q in range(19)]
RANK_Y = {
    q: [p for p in range(19) if VELOCITY[p][1] == VELOCITY[q][1]].index(q) for q in range(19)
}
RANK_Z = {
    q: [p for p in range(19) if VELOCITY[p][2] == VELOCITY[q][2]].index(q) for q in range(19)
}
NEIGHBOURS = sorted(
    (d for d in itertools.product((-1, 0, 1), repeat=3) if 1 <= sum(map(abs, d)) <= 2),
    key=lambda d: -sum(map(abs, d)),
)
ACROSS = [d for d in itertools.product((0,), (-1, 0, 1), (-1, 0, 1)) if any(d)]


def way(step):
    return 0 if step > 0 else 1


def neighbour(here, counts, offset):
    return tuple(
        lax.rem(place + step + count, count) if step else place
        for place, step, count in zip(here, offset, counts)
    )


def collide(f, solid, rate):
    total = {q: f[q] + f[q + 1] for q in range(1, 19, 2)}
    apart = {q: f[q] - f[q + 1] for q in range(1, 19, 2)}
    p_xy, p_xz, p_yz = total[7] + total[9], total[11] + total[13], total[15] + total[17]
    q_xy, q_xz, q_yz = total[7] - total[9], total[11] - total[13], total[15] - total[17]
    a_xy, b_xy = apart[7] + apart[9], apart[7] - apart[9]
    a_xz, b_xz = apart[11] + apart[13], apart[11] - apart[13]
    a_yz, b_yz = apart[15] + apart[17], apart[15] - apart[17]
    axis_sum = total[1] + total[3] + total[5]
    edge_sum = p_xy + p_xz + p_yz
    rho = f[0] + axis_sum + edge_sum
    far_x, far_y, far_z = a_xy + a_xz, b_xy + a_yz, b_xz + b_yz
    j_x, j_y, j_z = apart[1] + far_x, apart[3] + far_y, apart[5] + far_z
    inverse = 1.0 / rho
    u_x, u_y, u_z = j_x * inverse, j_y * inverse, j_z * inverse
    xx, yy, zz = j_x * u_x, j_y * u_y, j_z * u_z
    square = xx + yy + zz
    normal_xy, normal_z = xx - yy, 2.0 * zz - xx - yy

    def relax(which, norm, value):
        return (rate[which] * (1.0 / norm)) * value

    axis_xy, edge_xy = total[1] - total[3], p_xz - p_yz
    axis_z = 2.0 * total[5] - total[1] - total[3]
    edge_z = p_xz + p_yz - 2.0 * p_xy
    m4 = relax(0, 2394.0, 8.0 * edge_sum - 11.0 * axis_sum - 30.0 * f[0] + 11.0 * rho - 19.0 * square)
    m5 = relax(1, 12.0, axis_xy + edge_xy - normal_xy)
    m6 = relax(2, 36.0, axis_z + edge_z - normal_z)
    m7 = relax(3, 4.0, q_xy - j_x * u_y)
    m8 = relax(4, 4.0, q_yz - j_y * u_z)
    m9 = relax(5, 4.0, q_xz - j_x * u_z)
    m10 = relax(6, 40.0, far_x - 4.0 * apart[1] + (2.0 / 3.0) * j_x)
    m11 = relax(7, 40.0, far_y - 4.0 * apart[3] + (2.0 / 3.0) * j_y)
    m12 = relax(8, 40.0, far_z - 4.0 * apart[5] + (2.0 / 3.0) * j_z)
    m13 = relax(9, 8.0, a_xy - a_xz)
    m14 = relax(10, 8.0, a_yz - b_xy)
    m15 = relax(11, 8.0, b_xz - b_yz)
    m16 = relax(12, 252.0, 12.0 * f[0] - 4.0 * axis_sum + edge_sum - 3.0 * rho + 5.5 * square)
    m17 = relax(13, 24.0, edge_xy - 2.0 * axis_xy + 0.5 * normal_xy)
    m18 = relax(14, 72.0, edge_z - 2.0 * axis_z + 0.5 * normal_z)

    axis_base = -11.0 * m4 - 4.0 * m16
    edge_base = 8.0 * m4 + m16
    v5, v6 = m5 - 2.0 * m17, m6 - 2.0 * m18
    w5, w6 = m5 + m17, m6 + m18
    e_xy, e_xz, e_yz = edge_base - 2.0 * w6, edge_base + w5 + w6, edge_base - w5 + w6
    even = {
        1: axis_base + v5 - v6,
        3: axis_base - v5 - v6,
        5: axis_base + 2.0 * v6,
        7: e_xy + m7,
        9: e_xy - m7,
        11: e_xz + m9,
        13: e_xz - m9,
        15: e_yz + m8,
        17: e_yz - m8,
    }
    s_xy, t_xy = m10 + m13, m11 - m14
    s_xz, t_xz = m10 - m13, m12 + m15
    s_yz, t_yz = m11 + m14, m12 - m15
    odd = {
        1: -4.0 * m10,
        3: -4.0 * m11,
        5: -4.0 * m12,
        7: s_xy + t_xy,
        9: s_xy - t_xy,
        11: s_xz + t_xz,
        13: s_xz - t_xz,
        15: s_yz + t_yz,
        17: s_yz - t_yz,
    }
    post = [f[0] + 30.0 * m4 - 12.0 * m16]
    for q in range(1, 19, 2):
        post.append(f[q] - even[q] - odd[q])
        post.append(f[q + 1] - even[q] + odd[q])
    return [jnp.where(solid, f[OPPOSITE[q]], post[q]) for q in range(19)]


def inflow(turbulence):
    u = [0.05 + 0.05 * turbulence[0], 0.05 * turbulence[1], 0.05 * turbulence[2]]
    speed = 1.0 - 1.5 * (u[0] * u[0] + u[1] * u[1] + u[2] * u[2])
    result = []
    for q in range(19):
        weight = (1.0 / 3.0, 1.0 / 18.0, 1.0 / 36.0)[sum(map(abs, VELOCITY[q]))]
        along = None
        for step, part in zip(VELOCITY[q], u):
            if step:
                part = part if step > 0 else -part
                along = part if along is None else along + part
        result.append(weight * (speed if along is None else speed + along * (3.0 + 4.5 * along)))
    return result


def tap(offset, half_width):
    spread = half_width.astype(jnp.float32)
    reach = offset.astype(jnp.float32)
    value = jnp.exp(reach * reach * (-jnp.pi / (2.0 * (spread * spread))))
    return jnp.where(jnp.abs(reach) <= 2.0 * spread, value, 0.0)


def tap_norm(half_width):
    offset = lax.broadcasted_iota(jnp.int32, (8, 128), 1) - FILT
    value = jnp.where(offset <= FILT, tap(offset, half_width), 0.0)
    return 1.0 / jnp.sqrt(jnp.sum(value * value, axis=1, keepdims=True))[0:1]


def kernel(
    counts,
    f_hbm,
    rate_hbm,
    solid_hbm,
    noise_hbm,
    width_hbm,
    out,
    f_in,
    rate,
    solid,
    noise,
    width,
    post,
    send_y,
    send_z,
    from_y,
    from_z,
    from_yz,
    filter_y,
    filter_z,
    turbulence,
    load_sem,
    send_sem,
    recv_sem,
    noise_send,
    noise_recv,
):
    here = tuple(lax.axis_index(axis) for axis in AXES)
    at_inlet = here[0] == 0

    barrier = pltpu.get_barrier_semaphore()
    for offset in NEIGHBOURS:
        pl.semaphore_signal(
            barrier, inc=1, device_id=neighbour(here, counts, offset), device_id_type=MESH
        )

    loads = [
        pltpu.make_async_copy(f_hbm, f_in, load_sem.at[0]),
        pltpu.make_async_copy(rate_hbm, rate, load_sem.at[1]),
        pltpu.make_async_copy(solid_hbm, solid, load_sem.at[2]),
        pltpu.make_async_copy(noise_hbm, noise.at[1, 1], load_sem.at[3]),
        pltpu.make_async_copy(width_hbm, width, load_sem.at[4]),
    ]
    for load in loads:
        load.start()

    row = lax.broadcasted_iota(jnp.int32, (NY, NZ), 0)
    lane = lax.broadcasted_iota(jnp.int32, (NY, NZ), 1)

    def face_copies(slot):
        copies = []
        for number, offset in enumerate(NEIGHBOURS):
            dx, dy, dz = offset
            side = 0 if dx > 0 else 2 if dx < 0 else 1
            edge = NX - 1 if dx > 0 else 0
            if dx and not dy and not dz:
                group = pl.ds(0, 5) if dx > 0 else pl.ds(14, 5)
                source = post.at[slot, 1 + edge, group]
                target = post.at[slot, 0 if dx > 0 else NX + 1, group]
            elif dy and not dx and not dz:
                source = send_y.at[slot, way(dy)]
                target = from_y.at[slot, 1, way(dy)]
            elif dz and not dy:
                source = send_z.at[slot, way(dz)]
                target = from_z.at[slot, side, way(dz)]
            elif dx and dy:
                rank = RANK_Y[VELOCITY.index(offset)]
                source = send_y.at[slot, way(dy), edge, pl.ds(rank, 1)]
                target = from_y.at[slot, side, way(dy), edge, pl.ds(rank, 1)]
            else:
                source = send_z.at[slot, way(dz), pl.ds(NY - 1 if dy > 0 else 0, 1)]
                target = from_yz.at[slot, way(dy), way(dz), pl.ds(0, 1)]
            copies.append(
                pltpu.make_async_remote_copy(
                    src_ref=source,
                    dst_ref=target,
                    send_sem=send_sem.at[slot, number],
                    recv_sem=recv_sem.at[slot, number],
                    device_id=neighbour(here, counts, offset),
                    device_id_type=MESH,
                )
            )
        return copies

    def noise_copies(step):
        copies = []
        for number, offset in enumerate(ACROSS):
            block = pl.ds(step, 1)
            copies.append(
                pltpu.make_async_remote_copy(
                    src_ref=noise.at[1, 1, block],
                    dst_ref=noise.at[1 - offset[1], 1 - offset[2], block],
                    send_sem=noise_send.at[step, number],
                    recv_sem=noise_recv.at[step, number],
                    device_id=neighbour(here, counts, offset),
                    device_id_type=MESH,
                )
            )
        return copies

    def collide_plane(f, x, slot):
        result = collide(f, solid[x] > 0, [rate[k] for k in range(15)])
        for q in range(19):
            post[slot, x + 1, PLACE[q]] = result[q]
            step_y, step_z = VELOCITY[q][1:]
            if step_y:
                edge = NY - 1 if step_y > 0 else 0
                send_y[slot, way(step_y), x, RANK_Y[q] : RANK_Y[q] + 1] = result[q][edge : edge + 1]
        for step_z in (1, -1):
            packed = send_z[slot, way(step_z)]
            for q in range(19):
                if VELOCITY[q][2] == step_z:
                    mine = x * 8 + RANK_Z[q]
                    moved = pltpu.roll(result[q], mine + 1 if step_z > 0 else mine, 1)
                    packed = jnp.where(lane == mine, moved, packed)
            send_z[slot, way(step_z)] = packed

    def stream_plane(x, slot):
        result = []
        for q in range(19):
            step_x, step_y, step_z = VELOCITY[q]
            source = x - step_x
            value = post[slot, source + 1, PLACE[q]]
            if step_x:
                side = (source + 4) // 4
                source = source + 4 - 4 * side
            else:
                side = 1
            edge_y = 0 if step_y > 0 else NY - 1
            edge_z = 0 if step_z > 0 else NZ - 1
            line = None
            if step_y:
                line = from_y[slot, side, way(step_y), source, RANK_Y[q] : RANK_Y[q] + 1]
                line = jnp.broadcast_to(line, (NY, NZ))
            if step_z:
                turn = edge_z + 128 - (source * 8 + RANK_Z[q])
                turn = jnp.where(turn >= 128, turn - 128, turn)
                spin = 1 if step_z > 0 else NZ - 1
                value = jnp.where(
                    lane == edge_z,
                    pltpu.roll(from_z[slot, side, way(step_z)], turn, 1),
                    pltpu.roll(value, spin, 1),
                )
                if step_y:
                    point = from_yz[slot, way(step_y), way(step_z), 0:1]
                    point = jnp.broadcast_to(point, (NY, NZ))
                    line = jnp.where(
                        lane == edge_z, pltpu.roll(point, turn, 1), pltpu.roll(line, spin, 1)
                    )
            if step_y:
                spin = 1 if step_y > 0 else NY - 1
                value = jnp.where(row == edge_y, line, pltpu.roll(value, spin, 0))
            result.append(value)
        return result

    def inlet_plane(step, x, f):
        flow = inflow([turbulence[step, a] for a in range(3)])
        here_too = jnp.logical_and(at_inlet, x == 0)
        return [jnp.where(here_too, flow[q], f[q]) for q in range(19)]

    def filter_step(step):
        for copy in noise_copies(step):
            copy.wait_recv()

        def component(a, carry):
            across = jnp.concatenate(
                [
                    jnp.dot(
                        filter_y[a],
                        jnp.concatenate([noise[b, c, step, a] for b in range(3)], 0),
                        precision=lax.Precision.HIGHEST,
                        preferred_element_type=jnp.float32,
                    )
                    for c in range(3)
                ],
                1,
            )
            turbulence[step, a] = jnp.dot(
                across,
                filter_z[a],
                precision=lax.Precision.HIGHEST,
                preferred_element_type=jnp.float32,
            )
            return carry

        lax.fori_loop(0, 3, component, 0)

    turbulence[...] = jnp.zeros_like(turbulence)
    send_z[...] = jnp.zeros_like(send_z)

    loads[0].wait()
    loads[1].wait()
    loads[2].wait()

    def first(x, carry):
        collide_plane([f_in[q, x] for q in range(19)], x, 0)
        return carry

    lax.fori_loop(0, NX, first, 0)
    loads[3].wait()
    loads[4].wait()

    @pl.when(at_inlet)
    def _():
        def component(a, carry):
            reach_y = lax.broadcasted_iota(jnp.int32, (NY, 3 * NY), 1) - lax.broadcasted_iota(
                jnp.int32, (NY, 3 * NY), 0
            )
            filter_y[a] = tap(reach_y - NY, width[a, 0]) * tap_norm(width[a, 0])
            reach_z = lax.broadcasted_iota(jnp.int32, (3 * NZ, NZ), 0) - lax.broadcasted_iota(
                jnp.int32, (3 * NZ, NZ), 1
            )
            filter_z[a] = tap(reach_z - NZ, width[a, 1]) * tap_norm(width[a, 1])
            return carry

        lax.fori_loop(0, 3, component, 0)

    pl.semaphore_wait(barrier, len(NEIGHBOURS))

    for copy in face_copies(0):
        copy.start()

    @pl.when(at_inlet)
    def _():
        for step in range(STEPS):
            for copy in noise_copies(step):
                copy.start()

    def middle(step, carry):
        @pl.when(at_inlet)
        def _():
            filter_step(step)

        for copy in face_copies(step):
            copy.wait_recv()

        def plane(x, carry):
            collide_plane(inlet_plane(step, x, stream_plane(x, step)), x, step + 1)
            return carry

        lax.fori_loop(0, NX, plane, 0)
        for copy in face_copies(step + 1):
            copy.start()
        return carry

    lax.fori_loop(0, STEPS - 1, middle, 0)

    @pl.when(at_inlet)
    def _():
        filter_step(STEPS - 1)

    for copy in face_copies(STEPS - 1):
        copy.wait_recv()

    def last(x, carry):
        f = inlet_plane(STEPS - 1, x, stream_plane(x, STEPS - 1))
        for q in range(19):
            out[q, x] = f[q]
        return carry

    lax.fori_loop(0, NX, last, 0)

    for step in range(STEPS):
        for copy in face_copies(step):
            copy.wait_send()

    @pl.when(at_inlet)
    def _():
        for step in range(STEPS):
            for copy in noise_copies(step):
                copy.wait_send()


def solution(mesh):
    counts = tuple(mesh.shape[axis] for axis in AXES)
    number = len(NEIGHBOURS)
    tile = (NY, NZ)

    def local(populations_in, relax_rates, solid_mask, noise_slabs, half_widths):
        return pl.pallas_call(
            functools.partial(kernel, counts),
            name="lattice_steps",
            out_shape=jax.ShapeDtypeStruct(populations_in.shape, jnp.float32),
            in_specs=[pl.BlockSpec(memory_space=pltpu.HBM)] * 5,
            out_specs=pl.BlockSpec(memory_space=pltpu.VMEM),
            scratch_shapes=[
                pltpu.VMEM((19, NX) + tile, jnp.float32),
                pltpu.SMEM((15,), jnp.float32),
                pltpu.VMEM((NX,) + tile, jnp.int32),
                pltpu.VMEM((3, 3, STEPS, 3) + tile, jnp.float32),
                pltpu.SMEM((3, 2), jnp.int32),
                pltpu.VMEM((STEPS, NX + 2, 19) + tile, jnp.float32),
                pltpu.VMEM((STEPS, 2, NX) + tile, jnp.float32),
                pltpu.VMEM((STEPS, 2) + tile, jnp.float32),
                pltpu.VMEM((STEPS, 3, 2, NX) + tile, jnp.float32),
                pltpu.VMEM((STEPS, 3, 2) + tile, jnp.float32),
                pltpu.VMEM((STEPS, 2, 2) + tile, jnp.float32),
                pltpu.VMEM((3, NY, 3 * NY), jnp.float32),
                pltpu.VMEM((3, 3 * NZ, NZ), jnp.float32),
                pltpu.VMEM((STEPS, 3) + tile, jnp.float32),
                pltpu.SemaphoreType.DMA((5,)),
                pltpu.SemaphoreType.DMA((STEPS, number)),
                pltpu.SemaphoreType.DMA((STEPS, number)),
                pltpu.SemaphoreType.DMA((STEPS, len(ACROSS))),
                pltpu.SemaphoreType.DMA((STEPS, len(ACROSS))),
            ],
            compiler_params=pltpu.CompilerParams(
                collective_id=0, has_side_effects=True, vmem_limit_bytes=24 << 20
            ),
        )(populations_in, relax_rates, solid_mask, noise_slabs, half_widths)

    return jax.shard_map(
        local,
        mesh=mesh,
        in_specs=(
            P(None, "gx", "gy", "gz"),
            P(),
            P("gx", "gy", "gz"),
            P(None, None, "gy", "gz"),
            P(),
        ),
        out_specs=P(None, "gx", "gy", "gz"),
        check_vma=False,
    )
```

time: 173 us -> 44.2 us (0.26); the launches traced: 170 us -> 43.9 us
  starting transfers between devices: 115 us -> 0 us
  Pallas kernels: 0 us -> 39.9 us
  waiting for transfers between devices: 21.9 us -> 0 us
  local copies, waits for them, and re-layouts: 18.8 us -> 3.99 us
  matrix products: 7.83 us -> 0 us
  other arithmetic: 5.21 us -> 0 us
    ppermute x28 -> x0, starting transfers between devices: 115 us -> none  [the longest x14 71.6 us: with_halo(): lax.ppermute(head, axis, [((i + 1) % count, i) for i in range(count)])]
    pallas_call x0 -> x1, Pallas kernels: none -> 39.9 us  [local(): pl.pallas_call(functools.partial(kernel, counts), name='lattice_steps', o...]
    ppermute x28 -> x0, waiting for transfers between devices: 21.9 us -> none  [the longest x14 21.2 us: with_halo(): lax.ppermute(tail, axis, [(i, (i + 1) % count) for i in range(count)])]
    dot_general x17 -> x0, matrix products: 7.83 us -> none  [the longest x8 3.46 us: equilibrium(): jnp.einsum('qa,a...->q...', speeds, vel_field, precision=lax.Precision.HI...]
    slice x21 -> x0, local copies, waits for them, and re-layouts: 6.61 us -> none  [the longest x12 2.92 us: with_halo(): head = lax.slice_in_dim(cells, 0, width, axis=dim)]
    ppermute x8 -> x0, local copies, waits for them, and re-layouts: 3.88 us -> none  [the longest x4 1.94 us: with_halo(): lax.ppermute(tail, axis, [(i, (i + 1) % count) for i in range(count)])]
    another operation x8 -> x0, local copies, waits for them, and re-layouts: 3.79 us -> none  [the longest x4 1.89 us: collide(): bounced = jnp.stack([populations[int(which)] for which in opposite()])]
    concatenate x21 -> x0, other arithmetic: 2.4 us -> none  [with_halo(): jnp.concatenate([lax.ppermute(tail, axis, [(i, (i + 1) % count) for i in...]
  transfers between devices with their start and end apart: 28 -> 0, of which waited for: 16 -> 0; matrix products, arithmetic and copies ran while one was open for 7% -> 0% of each run, Pallas kernels for 0% -> 0%
where the time goes in v1:
time: 44.2 us; the launch traced here: 43.9 us
  Pallas kernels  39.9 us (90%)
  local copies, waits for them, and re-layouts  3.99 us (9%)
    pallas_call x1, Pallas kernels, local(): pl.pallas_call(functools.partial(kernel, counts), name='lattice_steps', o...  39.9 us
    unnamed x10, local copies, waits for them, and re-layouts  3.99 us

profile of v1, /device:TPU:1, one launch (start us, length us, event | category | flops | bytes accessed | tf_op | source)
XLA Modules:
  0.0 43.9 jit_solution(17840560444728132518)
XLA Ops:
  0.0 0.0 copy-start.3
  0.0 0.8 %copy.6.width_hbm = s32[3,2]{1,0:T(4,128)S(1)} copy(s32[3,2]{0,1:T(2,128)} %param.9) | data formatting | bytes 48 | tf_op args[4]
  0.8 0.0 copy-done.3
  0.8 0.0 copy-start
  0.8 1.0 %copy-done = f32[19,4,8,128]{3,2,1,0:T(8,128)S(1)} copy-done((f32[19,4,8,128]{3,2,1,0:T(8,128)S(1)}, f32[19,4,8,128]{3,2,1,0:T(8,128)}, u32[]{:S(2)}) %copy-start) | copy-done | bytes 311320
  1.8 0.0 copy-start.1
  1.8 0.8 %copy-done.1 = f32[4,3,8,128]{3,2,1,0:T(8,128)S(1)} copy-done((f32[4,3,8,128]{3,2,1,0:T(8,128)S(1)}, f32[4,3,8,128]{3,2,1,0:T(8,128)}, u32[]{:S(2)}) %copy-start.1) | copy-done | bytes 49176
  2.6 0.0 copy-start.2
  2.6 0.7 %copy-done.2 = s32[4,8,128]{2,1,0:T(8,128)S(1)} copy-done((s32[4,8,128]{2,1,0:T(8,128)S(1)}, s32[4,8,128]{2,1,0:T(8,128)}, u32[]{:S(2)}) %copy-start.2) | copy-done | bytes 16408
  3.3 39.9 %lattice_steps.1 = f32[19,4,8,128]{3,2,1,0:T(8,128)S(1)} custom-call(f32[19,4,8,128]{3,2,1,0:T(8,128)S(1)} %copy-done, f32[15]{0:T(128)S(1)} %copy-done.3, s32[4,8,128]{2,1,0:T(8,128)S(1)} %copy-done.2, f32[4,3,8,128]{3,2,1,0:T(8,128)S(1)} %copy-done.1, s32[3,2]{1,0:T(4,128)S(1)} %copy.6.width_hbm), custom_call_target="tpu_custom_call" | custom-call | tf_op jit(solution)/shard_map/lattice_steps/pallas_call | solution.py:450
  43.2 0.7 %copy.8 = f32[19,4,8,128]{3,2,1,0:T(8,128)} copy(f32[19,4,8,128]{3,2,1,0:T(8,128)S(1)} %lattice_steps.1) | data formatting | bytes 622592
Async XLA Ops:
  0.0 0.8 %copy-start.3 = (f32[15]{0:T(128)S(1)}, f32[15]{0:T(128)}, u32[]{:S(2)}) copy-start(f32[15]{0:T(128)} %rate_hbm.1) | copy-start | bytes 184
  0.8 1.0 %copy-start = (f32[19,4,8,128]{3,2,1,0:T(8,128)S(1)}, f32[19,4,8,128]{3,2,1,0:T(8,128)}, u32[]{:S(2)}) copy-start(f32[19,4,8,128]{3,2,1,0:T(8,128)} %f_hbm.1) | copy-start | bytes 933892
  1.8 0.8 %copy-start.1 = (f32[4,3,8,128]{3,2,1,0:T(8,128)S(1)}, f32[4,3,8,128]{3,2,1,0:T(8,128)}, u32[]{:S(2)}) copy-start(f32[4,3,8,128]{3,2,1,0:T(8,128)} %noise_hbm.1) | copy-start | bytes 147460
  2.6 0.7 %copy-start.2 = (s32[4,8,128]{2,1,0:T(8,128)S(1)}, s32[4,8,128]{2,1,0:T(8,128)}, u32[]{:S(2)}) copy-start(s32[4,8,128]{2,1,0:T(8,128)} %solid_hbm.1) | copy-start | bytes 49156

commit v2 on v1

--- a/solution.py
+++ b/solution.py
@@ -11,6 +11,7 @@
 MESH = pl.DeviceIdType.MESH
 AXES = ("gx", "gy", "gz")
 FILT = 8
+UNROLL = (4, 4, 4, 3)
 STEPS = 4
 NX, NY, NZ = 4, 8, 128
 VELOCITY = [
@@ -47,6 +48,8 @@
     (d for d in itertools.product((-1, 0, 1), repeat=3) if 1 <= sum(map(abs, d)) <= 2),
     key=lambda d: -sum(map(abs, d)),
 )
+FACE_TILES = 2 * 5 + 2 * NX + 2 + 4 + 1
+NOISE_TILES = 8 * 3
 ACROSS = [d for d in itertools.product((0,), (-1, 0, 1), (-1, 0, 1)) if any(d)]
 
 
@@ -192,8 +195,8 @@
     load_sem,
     send_sem,
     recv_sem,
-    noise_send,
     noise_recv,
+    ruler,
 ):
     here = tuple(lax.axis_index(axis) for axis in AXES)
     at_inlet = here[0] == 0
@@ -204,22 +207,26 @@
             barrier, inc=1, device_id=neighbour(here, counts, offset), device_id_type=MESH
         )
 
-    loads = [
-        pltpu.make_async_copy(f_hbm, f_in, load_sem.at[0]),
-        pltpu.make_async_copy(rate_hbm, rate, load_sem.at[1]),
-        pltpu.make_async_copy(solid_hbm, solid, load_sem.at[2]),
-        pltpu.make_async_copy(noise_hbm, noise.at[1, 1], load_sem.at[3]),
-        pltpu.make_async_copy(width_hbm, width, load_sem.at[4]),
-    ]
+    loads = [pltpu.make_async_copy(rate_hbm, rate, load_sem.at[NX])]
+    loads.append(pltpu.make_async_copy(solid_hbm, solid, load_sem.at[NX + 1]))
+    for x in range(NX):
+        plane = pl.ds(x, 1)
+        loads.append(pltpu.make_async_copy(f_hbm.at[:, plane], f_in.at[:, plane], load_sem.at[x]))
+    loads.append(pltpu.make_async_copy(width_hbm, width, load_sem.at[NX + 2]))
+    loads.append(pltpu.make_async_copy(noise_hbm, noise.at[1, 1], load_sem.at[NX + 3]))
     for load in loads:
         load.start()
 
     row = lax.broadcasted_iota(jnp.int32, (NY, NZ), 0)
     lane = lax.broadcasted_iota(jnp.int32, (NY, NZ), 1)
 
+    def await_bytes(tiles, semaphore):
+        span = ruler.at[pl.ds(0, tiles)]
+        pltpu.make_async_copy(span, span, semaphore).wait()
+
     def face_copies(slot):
         copies = []
-        for number, offset in enumerate(NEIGHBOURS):
+        for offset in NEIGHBOURS:
             dx, dy, dz = offset
             side = 0 if dx > 0 else 2 if dx < 0 else 1
             edge = NX - 1 if dx > 0 else 0
@@ -244,8 +251,8 @@
                 pltpu.make_async_remote_copy(
                     src_ref=source,
                     dst_ref=target,
-                    send_sem=send_sem.at[slot, number],
-                    recv_sem=recv_sem.at[slot, number],
+                    send_sem=send_sem.at[0],
+                    recv_sem=recv_sem.at[slot],
                     device_id=neighbour(here, counts, offset),
                     device_id_type=MESH,
                 )
@@ -254,14 +261,14 @@
 
     def noise_copies(step):
         copies = []
-        for number, offset in enumerate(ACROSS):
+        for offset in ACROSS:
             block = pl.ds(step, 1)
             copies.append(
                 pltpu.make_async_remote_copy(
                     src_ref=noise.at[1, 1, block],
                     dst_ref=noise.at[1 - offset[1], 1 - offset[2], block],
-                    send_sem=noise_send.at[step, number],
-                    recv_sem=noise_recv.at[step, number],
+                    send_sem=send_sem.at[1],
+                    recv_sem=noise_recv.at[step],
                     device_id=neighbour(here, counts, offset),
                     device_id_type=MESH,
                 )
@@ -329,8 +336,7 @@
         return [jnp.where(here_too, flow[q], f[q]) for q in range(19)]
 
     def filter_step(step):
-        for copy in noise_copies(step):
-            copy.wait_recv()
+        await_bytes(NOISE_TILES, noise_recv.at[step])
 
         def component(a, carry):
             across = jnp.concatenate(
@@ -353,22 +359,23 @@
             )
             return carry
 
-        lax.fori_loop(0, 3, component, 0)
+        lax.fori_loop(0, 3, component, 0, unroll=UNROLL[3])
 
     turbulence[...] = jnp.zeros_like(turbulence)
     send_z[...] = jnp.zeros_like(send_z)
 
     loads[0].wait()
     loads[1].wait()
-    loads[2].wait()
 
     def first(x, carry):
+        plane = pl.ds(x, 1)
+        pltpu.make_async_copy(f_hbm.at[:, plane], f_in.at[:, plane], load_sem.at[x]).wait()
         collide_plane([f_in[q, x] for q in range(19)], x, 0)
         return carry
 
-    lax.fori_loop(0, NX, first, 0)
-    loads[3].wait()
-    loads[4].wait()
+    lax.fori_loop(0, NX, first, 0, unroll=UNROLL[0])
+    loads[NX + 2].wait()
+    loads[NX + 3].wait()
 
     @pl.when(at_inlet)
     def _():
@@ -376,11 +383,11 @@
             reach_y = lax.broadcasted_iota(jnp.int32, (NY, 3 * NY), 1) - lax.broadcasted_iota(
                 jnp.int32, (NY, 3 * NY), 0
             )
-            filter_y[a] = tap(reach_y - NY, width[a, 0]) * tap_norm(width[a, 0])
+            filter_y[a] = tap(reach_y - NY, width[0, a]) * tap_norm(width[0, a])
             reach_z = lax.broadcasted_iota(jnp.int32, (3 * NZ, NZ), 0) - lax.broadcasted_iota(
                 jnp.int32, (3 * NZ, NZ), 1
             )
-            filter_z[a] = tap(reach_z - NZ, width[a, 1]) * tap_norm(width[a, 1])
+            filter_z[a] = tap(reach_z - NZ, width[1, a]) * tap_norm(width[1, a])
             return carry
 
         lax.fori_loop(0, 3, component, 0)
@@ -401,14 +408,13 @@
         def _():
             filter_step(step)
 
-        for copy in face_copies(step):
-            copy.wait_recv()
+        await_bytes(FACE_TILES, recv_sem.at[step])
 
         def plane(x, carry):
             collide_plane(inlet_plane(step, x, stream_plane(x, step)), x, step + 1)
             return carry
 
-        lax.fori_loop(0, NX, plane, 0)
+        lax.fori_loop(0, NX, plane, 0, unroll=UNROLL[1])
         for copy in face_copies(step + 1):
             copy.start()
         return carry
@@ -419,8 +425,7 @@
     def _():
         filter_step(STEPS - 1)
 
-    for copy in face_copies(STEPS - 1):
-        copy.wait_recv()
+    await_bytes(FACE_TILES, recv_sem.at[STEPS - 1])
 
     def last(x, carry):
         f = inlet_plane(STEPS - 1, x, stream_plane(x, STEPS - 1))
@@ -428,25 +433,21 @@
             out[q, x] = f[q]
         return carry
 
-    lax.fori_loop(0, NX, last, 0)
-
-    for step in range(STEPS):
-        for copy in face_copies(step):
-            copy.wait_send()
+    lax.fori_loop(0, NX, last, 0, unroll=UNROLL[2])
+
+    await_bytes(STEPS * FACE_TILES, send_sem.at[0])
 
     @pl.when(at_inlet)
     def _():
-        for step in range(STEPS):
-            for copy in noise_copies(step):
-                copy.wait_send()
+        await_bytes(STEPS * NOISE_TILES, send_sem.at[1])
 
 
 def solution(mesh):
     counts = tuple(mesh.shape[axis] for axis in AXES)
-    number = len(NEIGHBOURS)
     tile = (NY, NZ)
 
     def local(populations_in, relax_rates, solid_mask, noise_slabs, half_widths):
+        operands = (populations_in, relax_rates, solid_mask, noise_slabs, half_widths.T)
         return pl.pallas_call(
             functools.partial(kernel, counts),
             name="lattice_steps",
@@ -458,7 +459,7 @@
                 pltpu.SMEM((15,), jnp.float32),
                 pltpu.VMEM((NX,) + tile, jnp.int32),
                 pltpu.VMEM((3, 3, STEPS, 3) + tile, jnp.float32),
-                pltpu.SMEM((3, 2), jnp.int32),
+                pltpu.SMEM((2, 3), jnp.int32),
                 pltpu.VMEM((STEPS, NX + 2, 19) + tile, jnp.float32),
                 pltpu.VMEM((STEPS, 2, NX) + tile, jnp.float32),
                 pltpu.VMEM((STEPS, 2) + tile, jnp.float32),
@@ -468,16 +469,16 @@
                 pltpu.VMEM((3, NY, 3 * NY), jnp.float32),
                 pltpu.VMEM((3, 3 * NZ, NZ), jnp.float32),
                 pltpu.VMEM((STEPS, 3) + tile, jnp.float32),
-                pltpu.SemaphoreType.DMA((5,)),
-                pltpu.SemaphoreType.DMA((STEPS, number)),
-                pltpu.SemaphoreType.DMA((STEPS, number)),
-                pltpu.SemaphoreType.DMA((STEPS, len(ACROSS))),
-                pltpu.SemaphoreType.DMA((STEPS, len(ACROSS))),
+                pltpu.SemaphoreType.DMA((NX + 4,)),
+                pltpu.SemaphoreType.DMA((2,)),
+                pltpu.SemaphoreType.DMA((STEPS,)),
+                pltpu.SemaphoreType.DMA((STEPS,)),
+                pltpu.VMEM((STEPS * FACE_TILES,) + tile, jnp.float32),
             ],
             compiler_params=pltpu.CompilerParams(
                 collective_id=0, has_side_effects=True, vmem_limit_bytes=24 << 20
             ),
-        )(populations_in, relax_rates, solid_mask, noise_slabs, half_widths)
+        )(*[pltpu.with_memory_space_constraint(x, pltpu.HBM) for x in operands])
 
     return jax.shard_map(
         local,

time: 44.2 us -> 36.7 us (0.83)
  Pallas kernels: 39.9 us -> 35.8 us
  local copies, waits for them, and re-layouts: 3.99 us -> 0.72 us
    pallas_call x1, Pallas kernels: 39.9 us -> 35.8 us  [local(): pl.pallas_call(functools.partial(kernel, counts), name='lattice_steps', o...]
    unnamed x10 -> x1, local copies, waits for them, and re-layouts: 3.99 us -> 0.72 us
where the time goes in v2:
time: 36.7 us; the launch traced here: 36.5 us
  Pallas kernels  35.8 us (98%)
  local copies, waits for them, and re-layouts  0.72 us (2%)
    pallas_call x1, Pallas kernels, local(): pl.pallas_call(functools.partial(kernel, counts), name='lattice_steps', o...  35.8 us

profile of v2, /device:TPU:1, one launch (start us, length us, event | category | flops | bytes accessed | tf_op | source)
XLA Modules:
  0.0 36.5 jit_solution(17706367257534784720)
XLA Ops:
  0.0 35.8 %lattice_steps.1 = f32[19,4,8,128]{3,2,1,0:T(8,128)S(1)} custom-call(f32[19,4,8,128]{3,2,1,0:T(8,128)} %f_hbm.1, f32[15]{0:T(128)} %rate_hbm.1, s32[4,8,128]{2,1,0:T(8,128)} %solid_hbm.1, f32[4,3,8,128]{3,2,1,0:T(8,128)} %noise_hbm.1, s32[2,3]{1,0:T(2,128)} %bitcast.1), custom_call_target="tpu_custom_call" | custom-call | tf_op jit(solution)/shard_map/lattice_steps/pallas_call | solution.py:451
  35.8 0.7 %copy.7 = f32[19,4,8,128]{3,2,1,0:T(8,128)} copy(f32[19,4,8,128]{3,2,1,0:T(8,128)S(1)} %lattice_steps.1) | data formatting | bytes 622592

commit v3 on v2

--- a/solution.py
+++ b/solution.py
@@ -48,8 +48,10 @@
     (d for d in itertools.product((-1, 0, 1), repeat=3) if 1 <= sum(map(abs, d)) <= 2),
     key=lambda d: -sum(map(abs, d)),
 )
-FACE_TILES = 2 * 5 + 2 * NX + 2 + 4 + 1
-NOISE_TILES = 8 * 3
+LEVEL, UP, DOWN = ([d for d in NEIGHBOURS if d[0] == step] for step in (0, 1, -1))
+UP_ROWS = 5 * NY + 2 * NY + 2
+FACE_ROWS = 2 * UP_ROWS + 2 * NX * NY + 2 * NY + 4
+NOISE_ROWS = 8 * 3 * NY
 ACROSS = [d for d in itertools.product((0,), (-1, 0, 1), (-1, 0, 1)) if any(d)]
 
 
@@ -195,17 +197,29 @@
     load_sem,
     send_sem,
     recv_sem,
+    recv_up,
     noise_recv,
+    ready_sem,
     ruler,
 ):
     here = tuple(lax.axis_index(axis) for axis in AXES)
     at_inlet = here[0] == 0
 
+    at_outlet = here[0] == counts[0] - 1
     barrier = pltpu.get_barrier_semaphore()
-    for offset in NEIGHBOURS:
+
+    def greet(offset, semaphore=barrier):
         pl.semaphore_signal(
-            barrier, inc=1, device_id=neighbour(here, counts, offset), device_id_type=MESH
+            semaphore, inc=1, device_id=neighbour(here, counts, offset), device_id_type=MESH
         )
+
+    for offset in LEVEL + DOWN:
+        greet(offset)
+
+    @pl.when(jnp.logical_not(at_outlet))
+    def _():
+        for offset in UP:
+            greet(offset)
 
     loads = [pltpu.make_async_copy(rate_hbm, rate, load_sem.at[NX])]
     loads.append(pltpu.make_async_copy(solid_hbm, solid, load_sem.at[NX + 1]))
@@ -220,13 +234,13 @@
     row = lax.broadcasted_iota(jnp.int32, (NY, NZ), 0)
     lane = lax.broadcasted_iota(jnp.int32, (NY, NZ), 1)
 
-    def await_bytes(tiles, semaphore):
-        span = ruler.at[pl.ds(0, tiles)]
+    def await_rows(rows, semaphore):
+        span = ruler.at[pl.ds(0, rows)]
         pltpu.make_async_copy(span, span, semaphore).wait()
 
-    def face_copies(slot):
+    def face_copies(slot, offsets):
         copies = []
-        for offset in NEIGHBOURS:
+        for offset in offsets:
             dx, dy, dz = offset
             side = 0 if dx > 0 else 2 if dx < 0 else 1
             edge = NX - 1 if dx > 0 else 0
@@ -251,13 +265,45 @@
                 pltpu.make_async_remote_copy(
                     src_ref=source,
                     dst_ref=target,
-                    send_sem=send_sem.at[0],
-                    recv_sem=recv_sem.at[slot],
+                    send_sem=send_sem.at[2 if dx > 0 else 0],
+                    recv_sem=(recv_up if dx > 0 else recv_sem).at[slot],
                     device_id=neighbour(here, counts, offset),
                     device_id_type=MESH,
                 )
             )
         return copies
+
+    def send_faces(slot):
+        for copy in face_copies(slot, LEVEL):
+            copy.start()
+
+        @pl.when(jnp.logical_not(at_outlet))
+        def _():
+            for copy in face_copies(slot, UP):
+                copy.start()
+
+        @pl.when(jnp.logical_not(at_inlet))
+        def _():
+            for copy in face_copies(slot, DOWN):
+                copy.start()
+
+        @pl.when(jnp.logical_and(at_inlet, slot > 0))
+        def _():
+            @pl.when(slot == 1)
+            def _():
+                pl.semaphore_wait(ready_sem, len(DOWN))
+                for copy in face_copies(0, DOWN):
+                    copy.start()
+
+            for copy in face_copies(slot, DOWN):
+                copy.start()
+
+    def await_faces(slot):
+        await_rows(FACE_ROWS - UP_ROWS, recv_sem.at[slot])
+
+        @pl.when(jnp.logical_not(at_inlet))
+        def _():
+            await_rows(UP_ROWS, recv_up.at[slot])
 
     def noise_copies(step):
         copies = []
@@ -336,7 +382,7 @@
         return [jnp.where(here_too, flow[q], f[q]) for q in range(19)]
 
     def filter_step(step):
-        await_bytes(NOISE_TILES, noise_recv.at[step])
+        await_rows(NOISE_ROWS, noise_recv.at[step])
 
         def component(a, carry):
             across = jnp.concatenate(
@@ -392,10 +438,14 @@
 
         lax.fori_loop(0, 3, component, 0)
 
-    pl.semaphore_wait(barrier, len(NEIGHBOURS))
-
-    for copy in face_copies(0):
-        copy.start()
+    pl.semaphore_wait(barrier, jnp.where(at_inlet, len(LEVEL) + len(UP), len(NEIGHBOURS)))
+
+    @pl.when(at_outlet)
+    def _():
+        for offset in UP:
+            greet(offset, ready_sem)
+
+    send_faces(0)
 
     @pl.when(at_inlet)
     def _():
@@ -408,15 +458,14 @@
         def _():
             filter_step(step)
 
-        await_bytes(FACE_TILES, recv_sem.at[step])
+        await_faces(step)
 
         def plane(x, carry):
             collide_plane(inlet_plane(step, x, stream_plane(x, step)), x, step + 1)
             return carry
 
         lax.fori_loop(0, NX, plane, 0, unroll=UNROLL[1])
-        for copy in face_copies(step + 1):
-            copy.start()
+        send_faces(step + 1)
         return carry
 
     lax.fori_loop(0, STEPS - 1, middle, 0)
@@ -425,7 +474,7 @@
     def _():
         filter_step(STEPS - 1)
 
-    await_bytes(FACE_TILES, recv_sem.at[STEPS - 1])
+    await_faces(STEPS - 1)
 
     def last(x, carry):
         f = inlet_plane(STEPS - 1, x, stream_plane(x, STEPS - 1))
@@ -435,11 +484,15 @@
 
     lax.fori_loop(0, NX, last, 0, unroll=UNROLL[2])
 
-    await_bytes(STEPS * FACE_TILES, send_sem.at[0])
+    await_rows(STEPS * (FACE_ROWS - UP_ROWS), send_sem.at[0])
+
+    @pl.when(jnp.logical_not(at_outlet))
+    def _():
+        await_rows(STEPS * UP_ROWS, send_sem.at[2])
 
     @pl.when(at_inlet)
     def _():
-        await_bytes(STEPS * NOISE_TILES, send_sem.at[1])
+        await_rows(STEPS * NOISE_ROWS, send_sem.at[1])
 
 
 def solution(mesh):
@@ -470,10 +523,12 @@
                 pltpu.VMEM((3, 3 * NZ, NZ), jnp.float32),
                 pltpu.VMEM((STEPS, 3) + tile, jnp.float32),
                 pltpu.SemaphoreType.DMA((NX + 4,)),
-                pltpu.SemaphoreType.DMA((2,)),
+                pltpu.SemaphoreType.DMA((3,)),
                 pltpu.SemaphoreType.DMA((STEPS,)),
                 pltpu.SemaphoreType.DMA((STEPS,)),
-                pltpu.VMEM((STEPS * FACE_TILES,) + tile, jnp.float32),
+                pltpu.SemaphoreType.DMA((STEPS,)),
+                pltpu.SemaphoreType.REGULAR,
+                pltpu.VMEM((STEPS * FACE_ROWS, NZ), jnp.float32),
             ],
             compiler_params=pltpu.CompilerParams(
                 collective_id=0, has_side_effects=True, vmem_limit_bytes=24 << 20

time: 36.7 us -> 31.1 us (0.85)
  the two profiles are of different devices: /device:TPU:1 before, /device:TPU:96 now
where the time goes in v3:
time: 31.1 us; the launch traced here: 30.9 us
  Pallas kernels  30.2 us (97%)
  local copies, waits for them, and re-layouts  0.72 us (2%)
    pallas_call x1, Pallas kernels, local(): pl.pallas_call(functools.partial(kernel, counts), name='lattice_steps', o...  30.2 us
    unnamed x1, local copies, waits for them, and re-layouts  0.72 us

profile of v3, /device:TPU:96, one launch (start us, length us, event | category | flops | bytes accessed | tf_op | source)
XLA Modules:
  0.0 30.9 jit_solution(10865286078571216044)
XLA Ops:
  0.0 30.2 %lattice_steps.1 = f32[19,4,8,128]{3,2,1,0:T(8,128)S(1)} custom-call(f32[19,4,8,128]{3,2,1,0:T(8,128)} %f_hbm.1, f32[15]{0:T(128)} %rate_hbm.1, s32[4,8,128]{2,1,0:T(8,128)} %solid_hbm.1, f32[4,3,8,128]{3,2,1,0:T(8,128)} %noise_hbm.1, s32[2,3]{1,0:T(2,128)} %bitcast.1), custom_call_target="tpu_custom_call" | custom-call | tf_op jit(solution)/shard_map/lattice_steps/pallas_call | solution.py:504
  30.2 0.7 %copy.7 = f32[19,4,8,128]{3,2,1,0:T(8,128)} copy(f32[19,4,8,128]{3,2,1,0:T(8,128)S(1)} %lattice_steps.1) | data formatting | bytes 622592

commit v4 on v3

v4 whole, which is shorter than its diff:
```python
import functools
import itertools

import jax
import jax.numpy as jnp
from jax import lax
from jax.experimental import pallas as pl
from jax.experimental.pallas import tpu as pltpu
from jax.sharding import PartitionSpec as P

MESH = pl.DeviceIdType.MESH
AXES = ("gx", "gy", "gz")
FILT = 8
STEPS = 4
NX, NY, NZ = 4, 8, 128
UNROLL = 6
VELOCITY = [
    (0, 0, 0),
    (1, 0, 0),
    (-1, 0, 0),
    (0, 1, 0),
    (0, -1, 0),
    (0, 0, 1),
    (0, 0, -1),
    (1, 1, 0),
    (-1, -1, 0),
    (1, -1, 0),
    (-1, 1, 0),
    (1, 0, 1),
    (-1, 0, -1),
    (1, 0, -1),
    (-1, 0, 1),
    (0, 1, 1),
    (0, -1, -1),
    (0, 1, -1),
    (0, -1, 1),
]
OPPOSITE = [0] + [q + 1 if q % 2 == 1 else q - 1 for q in range(1, 19)]
SOLID = 19
ORDER = sorted(range(20), key=lambda q: (tuple(-c for c in (VELOCITY + [(0, 0, 0)])[q][:2]), q))
PLACE = [ORDER.index(q) for q in range(20)]
WIDE = 2
HALVES = STEPS // WIDE
PLANES = NX + 2 * WIDE
PACKED = 3
NEIGHBOURS = sorted(
    (d for d in itertools.product((-1, 0, 1), repeat=3) if any(d)),
    key=lambda d: -sum(map(abs, d)),
)
LEVEL, UP, DOWN = ([d for d in NEIGHBOURS if d[0] == step] for step in (0, 1, -1))
ACROSS = [d for d in itertools.product((0,), (-1, 0, 1, 2), (-1, 0, 1)) if any(d)]
BEYOND = [d for d in ACROSS if d[1] == 2]


def pieces(offset):
    dx, dy, dz = offset
    rows = (0, NY) if not dy else (NY - WIDE, WIDE) if dy > 0 else (0, WIDE)
    if dz:
        return [rows]
    if dx > 0:
        return [(5, 1, 0, 15, 1, rows), (4, 1, 0, 5, 0, rows)]
    if dx < 0:
        return [(2, 1, 5, 15, 6, rows), (3, 1, 15, 5, 7, rows)]
    if dy > 0:
        return [(2, NX, 0, 12, 2, rows), (2, NX, 15, 4, 2, rows)]
    return [(2, NX, 1, 4, 2, rows), (2, NX, 8, 12, 2, rows)]


def rows_of(offsets):
    return sum(
        piece[1] * PACKED if len(piece) == 2 else piece[1] * piece[3] * piece[5][1]
        for offset in offsets
        for piece in pieces(offset)
    )


UP_ROWS = rows_of(UP)
OTHER_ROWS = rows_of(LEVEL + DOWN)
NOISE_ROWS = len(ACROSS) * 3 * NY


def neighbour(here, counts, offset):
    return tuple(
        lax.rem(place + step + count, count) if step else place
        for place, step, count in zip(here, offset, counts)
    )


def collide(f, solid, rate):
    total = {q: f[q] + f[q + 1] for q in range(1, 19, 2)}
    apart = {q: f[q] - f[q + 1] for q in range(1, 19, 2)}
    p_xy, p_xz, p_yz = total[7] + total[9], total[11] + total[13], total[15] + total[17]
    q_xy, q_xz, q_yz = total[7] - total[9], total[11] - total[13], total[15] - total[17]
    a_xy, b_xy = apart[7] + apart[9], apart[7] - apart[9]
    a_xz, b_xz = apart[11] + apart[13], apart[11] - apart[13]
    a_yz, b_yz = apart[15] + apart[17], apart[15] - apart[17]
    axis_sum = total[1] + total[3] + total[5]
    edge_sum = p_xy + p_xz + p_yz
    rho = f[0] + axis_sum + edge_sum
    far_x, far_y, far_z = a_xy + a_xz, b_xy + a_yz, b_xz + b_yz
    j_x, j_y, j_z = apart[1] + far_x, apart[3] + far_y, apart[5] + far_z
    inverse = 1.0 / rho
    u_x, u_y, u_z = j_x * inverse, j_y * inverse, j_z * inverse
    xx, yy, zz = j_x * u_x, j_y * u_y, j_z * u_z
    square = xx + yy + zz
    normal_xy, normal_z = xx - yy, 2.0 * zz - xx - yy

    def relax(which, norm, value):
        return (rate[which] * (1.0 / norm)) * value

    axis_xy, edge_xy = total[1] - total[3], p_xz - p_yz
    axis_z = 2.0 * total[5] - total[1] - total[3]
    edge_z = p_xz + p_yz - 2.0 * p_xy
    m4 = relax(0, 2394.0, 8.0 * edge_sum - 11.0 * axis_sum - 30.0 * f[0] + 11.0 * rho - 19.0 * square)
    m5 = relax(1, 12.0, axis_xy + edge_xy - normal_xy)
    m6 = relax(2, 36.0, axis_z + edge_z - normal_z)
    m7 = relax(3, 4.0, q_xy - j_x * u_y)
    m8 = relax(4, 4.0, q_yz - j_y * u_z)
    m9 = relax(5, 4.0, q_xz - j_x * u_z)
    m10 = relax(6, 40.0, far_x - 4.0 * apart[1] + (2.0 / 3.0) * j_x)
    m11 = relax(7, 40.0, far_y - 4.0 * apart[3] + (2.0 / 3.0) * j_y)
    m12 = relax(8, 40.0, far_z - 4.0 * apart[5] + (2.0 / 3.0) * j_z)
    m13 = relax(9, 8.0, a_xy - a_xz)
    m14 = relax(10, 8.0, a_yz - b_xy)
    m15 = relax(11, 8.0, b_xz - b_yz)
    m16 = relax(12, 252.0, 12.0 * f[0] - 4.0 * axis_sum + edge_sum - 3.0 * rho + 5.5 * square)
    m17 = relax(13, 24.0, edge_xy - 2.0 * axis_xy + 0.5 * normal_xy)
    m18 = relax(14, 72.0, edge_z - 2.0 * axis_z + 0.5 * normal_z)

    axis_base = -11.0 * m4 - 4.0 * m16
    edge_base = 8.0 * m4 + m16
    v5, v6 = m5 - 2.0 * m17, m6 - 2.0 * m18
    w5, w6 = m5 + m17, m6 + m18
    e_xy, e_xz, e_yz = edge_base - 2.0 * w6, edge_base + w5 + w6, edge_base - w5 + w6
    even = {
        1: axis_base + v5 - v6,
        3: axis_base - v5 - v6,
        5: axis_base + 2.0 * v6,
        7: e_xy + m7,
        9: e_xy - m7,
        11: e_xz + m9,
        13: e_xz - m9,
        15: e_yz + m8,
        17: e_yz - m8,
    }
    s_xy, t_xy = m10 + m13, m11 - m14
    s_xz, t_xz = m10 - m13, m12 + m15
    s_yz, t_yz = m11 + m14, m12 - m15
    odd = {
        1: -4.0 * m10,
        3: -4.0 * m11,
        5: -4.0 * m12,
        7: s_xy + t_xy,
        9: s_xy - t_xy,
        11: s_xz + t_xz,
        13: s_xz - t_xz,
        15: s_yz + t_yz,
        17: s_yz - t_yz,
    }
    post = [f[0] + 30.0 * m4 - 12.0 * m16]
    for q in range(1, 19, 2):
        post.append(f[q] - even[q] - odd[q])
        post.append(f[q + 1] - even[q] + odd[q])
    return [jnp.where(solid, f[OPPOSITE[q]], post[q]) for q in range(19)]


def inflow(turbulence):
    u = [0.05 + 0.05 * turbulence[0], 0.05 * turbulence[1], 0.05 * turbulence[2]]
    speed = 1.0 - 1.5 * (u[0] * u[0] + u[1] * u[1] + u[2] * u[2])
    result = []
    for q in range(19):
        weight = (1.0 / 3.0, 1.0 / 18.0, 1.0 / 36.0)[sum(map(abs, VELOCITY[q]))]
        along = None
        for step, part in zip(VELOCITY[q], u):
            if step:
                part = part if step > 0 else -part
                along = part if along is None else along + part
        result.append(weight * (speed if along is None else speed + along * (3.0 + 4.5 * along)))
    return result


def tap(offset, half_width):
    spread = half_width.astype(jnp.float32)
    reach = offset.astype(jnp.float32)
    value = jnp.exp(reach * reach * (-jnp.pi / (2.0 * (spread * spread))))
    return jnp.where(jnp.abs(reach) <= 2.0 * spread, value, 0.0)


def tap_norm(half_width):
    offset = lax.broadcasted_iota(jnp.int32, (8, 128), 1) - FILT
    value = jnp.where(offset <= FILT, tap(offset, half_width), 0.0)
    return 1.0 / jnp.sqrt(jnp.sum(value * value, axis=1, keepdims=True))[0:1]


def kernel(
    counts,
    f_hbm,
    rate_hbm,
    solid_hbm,
    noise_hbm,
    width_hbm,
    out,
    f_in,
    rate,
    solid,
    noise,
    width,
    post,
    side,
    later,
    later_side,
    send_z,
    from_z,
    filter_y,
    filter_z,
    turbulence,
    flow,
    load_sem,
    send_sem,
    recv_sem,
    recv_up,
    noise_recv,
    ready_sem,
    ruler,
):
    here = tuple(lax.axis_index(axis) for axis in AXES)
    at_inlet = here[0] == 0
    at_outlet = here[0] == counts[0] - 1
    at_edge = jnp.logical_or(at_inlet, at_outlet)
    barrier = pltpu.get_barrier_semaphore()

    def greet(offset, semaphore=barrier):
        pl.semaphore_signal(
            semaphore, inc=1, device_id=neighbour(here, counts, offset), device_id_type=MESH
        )

    for offset in DOWN + LEVEL:
        greet(offset)

    @pl.when(jnp.logical_not(at_outlet))
    def _():
        for offset in UP:
            greet(offset)

    @pl.when(at_edge)
    def _():
        for offset in BEYOND:
            greet(offset)

    loads = [pltpu.make_async_copy(rate_hbm, rate, load_sem.at[NX])]
    loads.append(pltpu.make_async_copy(solid_hbm, solid, load_sem.at[NX + 1]))
    for x in range(NX):
        plane = pl.ds(x, 1)
        loads.append(pltpu.make_async_copy(f_hbm.at[:, plane], f_in.at[:, plane], load_sem.at[x]))
    loads.append(pltpu.make_async_copy(width_hbm, width, load_sem.at[NX + 2]))
    loads.append(pltpu.make_async_copy(noise_hbm, noise.at[1, 1], load_sem.at[NX + 3]))
    for load in loads:
        load.start()

    row = lax.broadcasted_iota(jnp.int32, (NY, NZ), 0)
    lane = lax.broadcasted_iota(jnp.int32, (NY, NZ), 1)
    quarter = lane & 3

    def spin(value, amount, axis=1):
        amount = amount % value.shape[axis]
        return pltpu.roll(value, amount, axis) if amount else value

    def await_rows(rows, semaphore):
        span = ruler.at[pl.ds(0, rows)]
        pltpu.make_async_copy(span, span, semaphore).wait()

    def face_copies(half, offsets):
        copies = []
        for offset in offsets:
            dx, dy, dz = offset
            form = 1 if dy else 0
            for piece in pieces(offset):
                if dz:
                    rows = pl.ds(*piece)
                    source = send_z.at[half, :, rows]
                    target = from_z.at[half, 1 - dx, 0 if dz > 0 else 1, form, :, rows]
                else:
                    first, number, array, arrays, there, rows = piece
                    array, rows = pl.ds(array, arrays), pl.ds(*rows)
                    source = post.at[half, pl.ds(first, number), array, 0, rows]
                    target = post.at[half, pl.ds(there, number), array, form, rows]
                copies.append(
                    pltpu.make_async_remote_copy(
                        src_ref=source,
                        dst_ref=target,
                        send_sem=send_sem.at[2 if dx > 0 else 0],
                        recv_sem=(recv_up if dx > 0 else recv_sem).at[half],
                        device_id=neighbour(here, counts, offset),
                        device_id_type=MESH,
                    )
                )
        return copies

    def noise_copies(step):
        copies = []
        for offset in ACROSS:
            block = pl.ds(step, 1)
            copies.append(
                pltpu.make_async_remote_copy(
                    src_ref=noise.at[1, 1, block],
                    dst_ref=noise.at[(1 - offset[1]) % 4, 1 - offset[2], block],
                    send_sem=send_sem.at[1],
                    recv_sem=noise_recv.at[step],
                    device_id=neighbour(here, counts, offset),
                    device_id_type=MESH,
                )
            )
        return copies

    def send_faces(half):
        @pl.when(jnp.logical_not(at_outlet))
        def _():
            for copy in face_copies(half, UP):
                copy.start()

        if half == 0:

            @pl.when(jnp.logical_not(at_inlet))
            def _():
                for copy in face_copies(half, DOWN):
                    copy.start()

        else:
            for copy in face_copies(half, DOWN):
                copy.start()
        for copy in face_copies(half, LEVEL):
            copy.start()

    def await_faces(half):
        await_rows(OTHER_ROWS, recv_sem.at[half])

        @pl.when(jnp.logical_not(at_inlet))
        def _():
            await_rows(UP_ROWS, recv_up.at[half])

    def rates():
        return [rate[k] for k in range(15)]

    def collide_plane(f, x, half):
        blocked = solid[x] > 0
        result = collide(f, blocked, rates()) + [jnp.where(blocked, 1.0, 0.0)]
        packed = [send_z[half, k] for k in range(PACKED)]
        for q in range(20):
            post[half, x + WIDE, PLACE[q], 0] = result[q]
            tile, slot = PLACE[q] // 8, PLACE[q] % 8
            first = 16 * slot + 4 * x + 2
            moved = pltpu.roll(result[q], lax.rem(first + 2, NZ), 1)
            packed[tile] = jnp.where(((lane - first) & (NZ - 1)) < 4, moved, packed[tile])
        for k in range(PACKED):
            send_z[half, k] = packed[k]

    def unpack(half):
        for form in range(2):
            merged = [
                [
                    jnp.where(
                        quarter >= 2,
                        from_z[half, block, 0, form, k],
                        spin(from_z[half, block, 1, form, k], -4),
                    )
                    for k in range(PACKED)
                ]
                for block in range(3)
            ]
            for place in range(20):
                tile, slot = place // 8, place % 8
                below, own, above = (
                    spin(merged[block][tile], shift - 16 * slot)
                    for block, shift in enumerate((-8, 8, 24))
                )
                side[place, form] = jnp.where(lane < 8, below, jnp.where(lane < 24, own, above))

    def column(tile, plane, step_z):
        amount = (0 if step_z > 0 else NZ - 1) + 2 * NZ - (4 * plane + (3 if step_z > 0 else 0))
        return pltpu.roll(tile, lax.rem(amount, NZ), 1)

    def exchange_rows(main, edge, step_y):
        main, edge = spin(main, step_y, 0), spin(edge, step_y, 0)
        swap = row == (0 if step_y > 0 else NY - 1)
        return jnp.where(swap, edge, main), jnp.where(swap, main, edge)

    def stream_plane(plane, planes_of, sides_of, both):
        result = [[], []]
        for q in range(19):
            step_x, step_y, step_z = VELOCITY[q]
            source = plane - step_x
            forms = [0, 1] if both or step_y else [0]
            value = [planes_of(source, q, form) for form in forms]
            if step_z:
                enters = lane == (0 if step_z > 0 else NZ - 1)
                value = [
                    jnp.where(enters, column(sides_of(q, form), source, step_z), spin(value[form], step_z))
                    for form in forms
                ]
            if step_y:
                value = exchange_rows(value[0], value[1], step_y)
            result[0].append(value[0])
            if both:
                result[1].append(value[1])
        return result

    def stream_side(half):
        result = [[], []]
        for q in range(19):
            step_x, step_y, step_z = VELOCITY[q]
            value = []
            for form in range(2):
                moved = spin(side[PLACE[q], form], 4 * step_x + step_z)
                if step_z:
                    place, origin = (0, NZ - 1) if step_z > 0 else (3, 0)
                    outer = None
                    for plane in range(1, PLANES - 1):
                        source = plane - step_x
                        taken = spin(post[half, source, PLACE[q], form], 4 * plane + place - origin)
                        outer = taken if outer is None else jnp.where(lane >= 4 * plane, taken, outer)
                    moved = jnp.where(quarter == place, outer, moved)
                value.append(moved)
            if step_y:
                value = exchange_rows(value[0], value[1], step_y)
            for form in range(2):
                result[form].append(value[form])
        return result

    def filter_step(step):
        await_rows(NOISE_ROWS, noise_recv.at[step])

        def component(a, carry):
            across = jnp.concatenate(
                [
                    jnp.dot(
                        filter_y[a],
                        jnp.concatenate([noise[b, c, step, a] for b in range(4)], 0),
                        precision=lax.Precision.HIGHEST,
                        preferred_element_type=jnp.float32,
                    )
                    for c in range(3)
                ],
                1,
            )
            turbulence[step, a] = jnp.dot(
                across,
                filter_z[a],
                precision=lax.Precision.HIGHEST,
                preferred_element_type=jnp.float32,
            )
            return carry

        lax.fori_loop(0, 3, component, 0, unroll=3)
        for q, value in enumerate(inflow([turbulence[step, a] for a in range(3)])):
            flow[step % WIDE, q] = value

    def inflow_at(step, q, form, packed):
        return flow[step % WIDE, q, form * NY : (form + 1) * NY, packed * NZ : (packed + 1) * NZ]

    send_z[...] = jnp.zeros_like(send_z)
    loads[0].wait()
    loads[1].wait()

    def first(x, carry):
        plane = pl.ds(x, 1)
        pltpu.make_async_copy(f_hbm.at[:, plane], f_in.at[:, plane], load_sem.at[x]).wait()
        collide_plane([f_in[q, x] for q in range(19)], x, 0)
        return carry

    lax.fori_loop(0, NX, first, 0, unroll=NX)
    loads[NX + 2].wait()
    loads[NX + 3].wait()

    @pl.when(at_edge)
    def _():
        def component(a, carry):
            index = lax.broadcasted_iota(jnp.int32, (2 * NY, 4 * NY), 0)
            node = jnp.where(index < NY + 4, index, index - 2 * NY)
            node = jnp.where(jnp.logical_and(index >= NY, index < NY + 4), index, node)
            reach_y = lax.broadcasted_iota(jnp.int32, (2 * NY, 4 * NY), 1) - NY - node
            reach_y = jnp.where(reach_y > 2 * NY - 1, reach_y - 4 * NY, reach_y)
            filter_y[a] = tap(reach_y, width[0, a]) * tap_norm(width[0, a])
            index = lax.broadcasted_iota(jnp.int32, (3 * NZ, 2 * NZ), 1)
            part = index & 3
            node = jnp.where(index < NZ, index, jnp.where(part < 2, part + NZ, part - 4))
            reach_z = lax.broadcasted_iota(jnp.int32, (3 * NZ, 2 * NZ), 0) - NZ - node
            filter_z[a] = tap(reach_z, width[1, a]) * tap_norm(width[1, a])
            return carry

        lax.fori_loop(0, 3, component, 0)

    expected = jnp.where(at_inlet, len(LEVEL) + len(UP), len(NEIGHBOURS))
    pl.semaphore_wait(barrier, expected + jnp.where(at_edge, len(BEYOND), 0))

    @pl.when(at_outlet)
    def _():
        for offset in UP:
            greet(offset, ready_sem)

    for half in range(HALVES):
        send_faces(half)

        @pl.when(at_edge)
        def _():
            if half == 0:
                for step in range(STEPS):
                    for copy in noise_copies(step):
                        copy.start()

                @pl.when(at_inlet)
                def _():
                    pl.semaphore_wait(ready_sem, len(DOWN))
                    for copy in face_copies(0, DOWN):
                        copy.start()

            for step in range(WIDE * half, WIDE * half + WIDE):
                filter_step(step)

        await_faces(half)
        unpack(half)

        step = WIDE * half

        def around(index, carry):
            plane = index + 1
            f = stream_plane(
                plane,
                lambda source, q, form: post[half, source, PLACE[q], form],
                lambda q, form: side[PLACE[q], form],
                True,
            )
            set_here = jnp.logical_or(
                jnp.logical_and(at_inlet, plane == WIDE),
                jnp.logical_and(at_outlet, plane == WIDE + NX),
            )
            for form in range(2):
                f_form = [
                    jnp.where(set_here, inflow_at(step, q, form, 0), f[form][q]) for q in range(19)
                ]
                result = collide(f_form, post[half, plane, PLACE[SOLID], form] > 0.5, rates())
                for q in range(19):
                    later[index, q, form] = result[q]
            return carry

        lax.fori_loop(0, PLANES - 2, around, 0, unroll=UNROLL)
        f = stream_side(half)
        edge_plane = jnp.where(at_inlet, WIDE, WIDE + NX)
        set_here = jnp.logical_and(at_edge, (lane >> 2) == edge_plane)
        for form in range(2):
            f_form = [
                jnp.where(set_here, inflow_at(step, q, form, 1), f[form][q]) for q in range(19)
            ]
            result = collide(f_form, side[PLACE[SOLID], form] > 0.5, rates())
            for q in range(19):
                later_side[q, form] = result[q]

        step = WIDE * half + 1

        def own(x, carry):
            f = stream_plane(
                x + WIDE,
                lambda source, q, form: later[source - 1, q, form],
                lambda q, form: later_side[q, form],
                False,
            )[0]
            set_here = jnp.logical_and(at_inlet, x == 0)
            f = [jnp.where(set_here, inflow_at(step, q, 0, 0), f[q]) for q in range(19)]
            if half + 1 < HALVES:
                collide_plane(f, x, half + 1)
            else:
                for q in range(19):
                    out[q, x] = f[q]
            return carry

        lax.fori_loop(0, NX, own, 0, unroll=NX)

    await_rows(HALVES * OTHER_ROWS, send_sem.at[0])

    @pl.when(jnp.logical_not(at_outlet))
    def _():
        await_rows(HALVES * UP_ROWS, send_sem.at[2])

    @pl.when(at_edge)
    def _():
        await_rows(STEPS * NOISE_ROWS, send_sem.at[1])


def solution(mesh):
    counts = tuple(mesh.shape[axis] for axis in AXES)
    tile = (NY, NZ)

    def local(populations_in, relax_rates, solid_mask, noise_slabs, half_widths):
        operands = (populations_in, relax_rates, solid_mask, noise_slabs, half_widths.T)
        return pl.pallas_call(
            functools.partial(kernel, counts),
            name="lattice_steps",
            out_shape=jax.ShapeDtypeStruct(populations_in.shape, jnp.float32),
            in_specs=[pl.BlockSpec(memory_space=pltpu.HBM)] * 5,
            out_specs=pl.BlockSpec(memory_space=pltpu.VMEM),
            scratch_shapes=[
                pltpu.VMEM((19, NX) + tile, jnp.float32),
                pltpu.SMEM((15,), jnp.float32),
                pltpu.VMEM((NX,) + tile, jnp.int32),
                pltpu.VMEM((4, 3, STEPS, 3) + tile, jnp.float32),
                pltpu.SMEM((2, 3), jnp.int32),
                pltpu.VMEM((HALVES, PLANES, 20, 2) + tile, jnp.float32),
                pltpu.VMEM((20, 2) + tile, jnp.float32),
                pltpu.VMEM((PLANES - 2, 19, 2) + tile, jnp.float32),
                pltpu.VMEM((19, 2) + tile, jnp.float32),
                pltpu.VMEM((HALVES, PACKED) + tile, jnp.float32),
                pltpu.VMEM((HALVES, 3, 2, 2, PACKED) + tile, jnp.float32),
                pltpu.VMEM((3, 2 * NY, 4 * NY), jnp.float32),
                pltpu.VMEM((3, 3 * NZ, 2 * NZ), jnp.float32),
                pltpu.VMEM((STEPS, 3, 2 * NY, 2 * NZ), jnp.float32),
                pltpu.VMEM((WIDE, 19, 2 * NY, 2 * NZ), jnp.float32),
                pltpu.SemaphoreType.DMA((NX + 4,)),
                pltpu.SemaphoreType.DMA((3,)),
                pltpu.SemaphoreType.DMA((HALVES,)),
                pltpu.SemaphoreType.DMA((HALVES,)),
                pltpu.SemaphoreType.DMA((STEPS,)),
                pltpu.SemaphoreType.REGULAR,
                pltpu.VMEM((max(HALVES * OTHER_ROWS, STEPS * NOISE_ROWS), NZ), jnp.float32),
            ],
            compiler_params=pltpu.CompilerParams(
                collective_id=0, has_side_effects=True, vmem_limit_bytes=32 << 20
            ),
        )(*[pltpu.with_memory_space_constraint(x, pltpu.HBM) for x in operands])

    return jax.shard_map(
        local,
        mesh=mesh,
        in_specs=(
            P(None, "gx", "gy", "gz"),
            P(),
            P("gx", "gy", "gz"),
            P(None, None, "gy", "gz"),
            P(),
        ),
        out_specs=P(None, "gx", "gy", "gz"),
        check_vma=False,
    )
```

time: 31.1 us -> 29 us (0.932)
  the two profiles are of different devices: /device:TPU:96 before, /device:TPU:1 now
where the time goes in v4:
time: 29 us; the launch traced here: 28.8 us
  Pallas kernels  28.1 us (97%)
  local copies, waits for them, and re-layouts  0.72 us (2%)
    pallas_call x1, Pallas kernels, local(): pl.pallas_call(functools.partial(kernel, counts), name='lattice_steps', o...  28.1 us
    unnamed x1, local copies, waits for them, and re-layouts  0.72 us

profile of v4, /device:TPU:1, one launch (start us, length us, event | category | flops | bytes accessed | tf_op | source)
XLA Modules:
  0.0 28.8 jit_solution(12726237943454463728)
XLA Ops:
  0.0 28.1 %lattice_steps.1 = f32[19,4,8,128]{3,2,1,0:T(8,128)S(1)} custom-call(f32[19,4,8,128]{3,2,1,0:T(8,128)} %f_hbm.1, f32[15]{0:T(128)} %rate_hbm.1, s32[4,8,128]{2,1,0:T(8,128)} %solid_hbm.1, f32[4,3,8,128]{3,2,1,0:T(8,128)} %noise_hbm.1, s32[2,3]{1,0:T(2,128)} %bitcast.1), custom_call_target="tpu_custom_call" | custom-call | tf_op jit(solution)/shard_map/lattice_steps/pallas_call | solution.py:594
  28.1 0.7 %copy.7 = f32[19,4,8,128]{3,2,1,0:T(8,128)} copy(f32[19,4,8,128]{3,2,1,0:T(8,128)S(1)} %lattice_steps.1) | data formatting | bytes 622592

commit v5 on v4

--- a/solution.py
+++ b/solution.py
@@ -42,7 +42,8 @@
 WIDE = 2
 HALVES = STEPS // WIDE
 PLANES = NX + 2 * WIDE
-PACKED = 3
+RISING, SINKING = ([q for q in range(19) if VELOCITY[q][2] == step] for step in (1, -1))
+STAYING = [q for q in range(19) if VELOCITY[q][2] == 0] + [SOLID]
 NEIGHBOURS = sorted(
     (d for d in itertools.product((-1, 0, 1), repeat=3) if any(d)),
     key=lambda d: -sum(map(abs, d)),
@@ -54,29 +55,57 @@
 
 def pieces(offset):
     dx, dy, dz = offset
-    rows = (0, NY) if not dy else (NY - WIDE, WIDE) if dy > 0 else (0, WIDE)
     if dz:
-        return [rows]
+        return [(0, NY) if not dy else (NY - WIDE, WIDE) if dy > 0 else (0, WIDE)]
+    near_row, far_row = ((0, NY), None) if not dy else ((7, 1), (6, 1)) if dy > 0 else ((0, 1), (1, 1))
     if dx > 0:
-        return [(5, 1, 0, 15, 1, rows), (4, 1, 0, 5, 0, rows)]
-    if dx < 0:
-        return [(2, 1, 5, 15, 6, rows), (3, 1, 15, 5, 7, rows)]
-    if dy > 0:
-        return [(2, NX, 0, 12, 2, rows), (2, NX, 15, 4, 2, rows)]
-    return [(2, NX, 1, 4, 2, rows), (2, NX, 8, 12, 2, rows)]
+        whole = [
+            [[(0, 15)], []],
+            [[(0, 12)], [(0, 1), (5, 3)]],
+            [[(1, 4), (8, 7)], [(4, 1), (12, 3)]],
+        ][dy]
+        half = [[[(0, 5)], []], [[(0, 4)], [(0, 1)]], [[(1, 4)], [(4, 1)]]][dy]
+        planes = [(5, 1, 1, whole), (4, 1, 0, half)]
+    elif dx < 0:
+        whole = [
+            [[(5, 15)], []],
+            [[(5, 7), (15, 4)], [(5, 3), (15, 1)]],
+            [[(8, 12)], [(12, 3), (19, 1)]],
+        ][dy]
+        half = [[[(15, 5)], []], [[(15, 4)], [(15, 1)]], [[(16, 4)], [(19, 1)]]][dy]
+        planes = [(2, 1, 6, whole), (3, 1, 7, half)]
+    elif dy > 0:
+        planes = [(2, NX, 2, [[(0, 12), (15, 4)], [(0, 1), (5, 3), (15, 1)]])]
+    else:
+        planes = [(2, NX, 2, [[(1, 4), (8, 12)], [(4, 1), (12, 3), (19, 1)]])]
+    return [
+        (first, number, array, arrays, there, rows)
+        for first, number, there, ranges in planes
+        for rows, parts in zip((near_row, far_row), ranges)
+        for array, arrays in parts
+    ]
 
 
 def rows_of(offsets):
     return sum(
-        piece[1] * PACKED if len(piece) == 2 else piece[1] * piece[3] * piece[5][1]
+        piece[1] if len(piece) == 2 else piece[1] * piece[3] * piece[5][1]
         for offset in offsets
         for piece in pieces(offset)
     )
 
 
+SHORT, LONG = ([d for d in NEIGHBOURS if (d[2] != 0) == short] for short in (True, False))
 UP_ROWS = rows_of(UP)
 OTHER_ROWS = rows_of(LEVEL + DOWN)
-NOISE_ROWS = len(ACROSS) * 3 * NY
+
+
+def received(offsets, kind):
+    return rows_of([d for d in offsets if d in kind])
+
+
+REACH = 10
+NOISE_Y_ROWS = WIDE * 3 * (2 * NY + 2)
+NOISE_ROWS = [6 * NY + 2 * 2 + NOISE_Y_ROWS, NOISE_Y_ROWS]
 
 
 def neighbour(here, counts, offset):
@@ -204,6 +233,8 @@
     rate,
     solid,
     noise,
+    noise_z,
+    noise_side,
     width,
     post,
     side,
@@ -253,7 +284,7 @@
         plane = pl.ds(x, 1)
         loads.append(pltpu.make_async_copy(f_hbm.at[:, plane], f_in.at[:, plane], load_sem.at[x]))
     loads.append(pltpu.make_async_copy(width_hbm, width, load_sem.at[NX + 2]))
-    loads.append(pltpu.make_async_copy(noise_hbm, noise.at[1, 1], load_sem.at[NX + 3]))
+    loads.append(pltpu.make_async_copy(noise_hbm, noise.at[1], load_sem.at[NX + 3]))
     for load in loads:
         load.start()
 
@@ -277,8 +308,8 @@
             for piece in pieces(offset):
                 if dz:
                     rows = pl.ds(*piece)
-                    source = send_z.at[half, :, rows]
-                    target = from_z.at[half, 1 - dx, 0 if dz > 0 else 1, form, :, rows]
+                    source = send_z.at[half, 0 if dz > 0 else 1, rows]
+                    target = from_z.at[half, 1 - dx, 0 if dz > 0 else 1, form, rows]
                 else:
                     first, number, array, arrays, there, rows = piece
                     array, rows = pl.ds(array, arrays), pl.ds(*rows)
@@ -289,28 +320,46 @@
                         src_ref=source,
                         dst_ref=target,
                         send_sem=send_sem.at[2 if dx > 0 else 0],
-                        recv_sem=(recv_up if dx > 0 else recv_sem).at[half],
+                        recv_sem=(recv_up if dx > 0 else recv_sem).at[half, 0 if dz else 1],
                         device_id=neighbour(here, counts, offset),
                         device_id_type=MESH,
                     )
                 )
         return copies
 
-    def noise_copies(step):
+    def noise_copies(half):
         copies = []
         for offset in ACROSS:
-            block = pl.ds(step, 1)
-            copies.append(
-                pltpu.make_async_remote_copy(
-                    src_ref=noise.at[1, 1, block],
-                    dst_ref=noise.at[(1 - offset[1]) % 4, 1 - offset[2], block],
-                    send_sem=send_sem.at[1],
-                    recv_sem=noise_recv.at[step],
-                    device_id=neighbour(here, counts, offset),
-                    device_id_type=MESH,
+            dy, dz = offset[1:]
+            block, direction = (1 - dy) % 4, 0 if dz > 0 else 1
+            steps = pl.ds(WIDE * half, WIDE)
+            if dz and half:
+                continue
+            for rows in [(0, 1), (NY - 1, 1)] if offset in BEYOND else [(0, NY)]:
+                rows = pl.ds(*rows)
+                copies.append(
+                    pltpu.make_async_remote_copy(
+                        src_ref=noise_z.at[direction, rows] if dz else noise.at[1, steps, :, rows],
+                        dst_ref=noise_side.at[block, direction, rows]
+                        if dz
+                        else noise.at[block, steps, :, rows],
+                        send_sem=send_sem.at[1],
+                        recv_sem=noise_recv.at[half],
+                        device_id=neighbour(here, counts, offset),
+                        device_id_type=MESH,
+                    )
                 )
-            )
         return copies
+
+    def pack_noise():
+        above, below = jnp.zeros((NY, NZ), jnp.float32), jnp.zeros((NY, NZ), jnp.float32)
+        for k in range(3 * STEPS):
+            place = REACH * k
+            mine = jnp.logical_and(lane >= place, lane < place + REACH)
+            tile = noise[1, k // 3, k % 3]
+            above = jnp.where(mine, spin(tile, place + REACH), above)
+            below = jnp.where(mine, spin(tile, place), below)
+        noise_z[0], noise_z[1] = above, below
 
     def send_faces(half):
         @pl.when(jnp.logical_not(at_outlet))
@@ -318,25 +367,29 @@
             for copy in face_copies(half, UP):
                 copy.start()
 
-        if half == 0:
-
-            @pl.when(jnp.logical_not(at_inlet))
-            def _():
-                for copy in face_copies(half, DOWN):
-                    copy.start()
-
-        else:
+        @pl.when(jnp.logical_not(at_inlet))
+        def _():
             for copy in face_copies(half, DOWN):
                 copy.start()
+
         for copy in face_copies(half, LEVEL):
             copy.start()
-
-    def await_faces(half):
-        await_rows(OTHER_ROWS, recv_sem.at[half])
+        if half == 1:
+
+            @pl.when(at_inlet)
+            def _():
+                pl.semaphore_wait(ready_sem, len(DOWN))
+                for late in range(2):
+                    for copy in face_copies(late, DOWN):
+                        copy.start()
+
+    def await_faces(half, kind):
+        place = 0 if kind is SHORT else 1
+        await_rows(received(LEVEL + DOWN, kind), recv_sem.at[half, place])
 
         @pl.when(jnp.logical_not(at_inlet))
         def _():
-            await_rows(UP_ROWS, recv_up.at[half])
+            await_rows(received(UP, kind), recv_up.at[half, place])
 
     def rates():
         return [rate[k] for k in range(15)]
@@ -344,36 +397,43 @@
     def collide_plane(f, x, half):
         blocked = solid[x] > 0
         result = collide(f, blocked, rates()) + [jnp.where(blocked, 1.0, 0.0)]
-        packed = [send_z[half, k] for k in range(PACKED)]
         for q in range(20):
             post[half, x + WIDE, PLACE[q], 0] = result[q]
-            tile, slot = PLACE[q] // 8, PLACE[q] % 8
-            first = 16 * slot + 4 * x + 2
-            moved = pltpu.roll(result[q], lax.rem(first + 2, NZ), 1)
-            packed[tile] = jnp.where(((lane - first) & (NZ - 1)) < 4, moved, packed[tile])
-        for k in range(PACKED):
-            send_z[half, k] = packed[k]
+        above, below = send_z[half, 0], send_z[half, 1]
+        for k in range(5):
+            place = 16 * k + 4 * x
+            moved = pltpu.roll(result[RISING[k]], place + 4, 1)
+            above = jnp.where(jnp.logical_or(lane == place + 2, lane == place + 3), moved, above)
+            moved = pltpu.roll(result[SINKING[k]], place, 1)
+            below = jnp.where(jnp.logical_or(lane == place, lane == place + 1), moved, below)
+        for k in range(10):
+            place = 16 * (k // 2) + 4 * x + k % 2
+            above = jnp.where(lane == place, pltpu.roll(result[STAYING[k]], place + 1, 1), above)
+            place = place + 2
+            below = jnp.where(lane == place, pltpu.roll(result[STAYING[k]], place, 1), below)
+        send_z[half, 0], send_z[half, 1] = above, below
 
     def unpack(half):
         for form in range(2):
-            merged = [
-                [
-                    jnp.where(
-                        quarter >= 2,
-                        from_z[half, block, 0, form, k],
-                        spin(from_z[half, block, 1, form, k], -4),
-                    )
-                    for k in range(PACKED)
-                ]
-                for block in range(3)
-            ]
-            for place in range(20):
-                tile, slot = place // 8, place % 8
+            pairs, lone = [], ([], [])
+            for block in range(3):
+                low, high = from_z[half, block, 0, form], from_z[half, block, 1, form]
+                pairs.append(jnp.where(quarter >= 2, low, high))
+                for k in range(2):
+                    lone[k].append(jnp.where(quarter == 3, spin(low, 3 - k), spin(high, -2 - k)))
+
+            def spread(tiles, slot):
                 below, own, above = (
-                    spin(merged[block][tile], shift - 16 * slot)
-                    for block, shift in enumerate((-8, 8, 24))
+                    spin(tile, shift - 16 * slot) for tile, shift in zip(tiles, (-8, 8, 24))
                 )
-                side[place, form] = jnp.where(lane < 8, below, jnp.where(lane < 24, own, above))
+                return jnp.where(lane < 8, below, jnp.where(lane < 24, own, above))
+
+            for k in range(5):
+                tile = spread(pairs, k)
+                side[PLACE[RISING[k]], form] = tile
+                side[PLACE[SINKING[k]], form] = tile
+            for k in range(10):
+                side[PLACE[STAYING[k]], form] = spread(lone[k % 2], k // 2)
 
     def column(tile, plane, step_z):
         amount = (0 if step_z > 0 else NZ - 1) + 2 * NZ - (4 * plane + (3 if step_z > 0 else 0))
@@ -426,53 +486,7 @@
                 result[form].append(value[form])
         return result
 
-    def filter_step(step):
-        await_rows(NOISE_ROWS, noise_recv.at[step])
-
-        def component(a, carry):
-            across = jnp.concatenate(
-                [
-                    jnp.dot(
-                        filter_y[a],
-                        jnp.concatenate([noise[b, c, step, a] for b in range(4)], 0),
-                        precision=lax.Precision.HIGHEST,
-                        preferred_element_type=jnp.float32,
-                    )
-                    for c in range(3)
-                ],
-                1,
-            )
-            turbulence[step, a] = jnp.dot(
-                across,
-                filter_z[a],
-                precision=lax.Precision.HIGHEST,
-                preferred_element_type=jnp.float32,
-            )
-            return carry
-
-        lax.fori_loop(0, 3, component, 0, unroll=3)
-        for q, value in enumerate(inflow([turbulence[step, a] for a in range(3)])):
-            flow[step % WIDE, q] = value
-
-    def inflow_at(step, q, form, packed):
-        return flow[step % WIDE, q, form * NY : (form + 1) * NY, packed * NZ : (packed + 1) * NZ]
-
-    send_z[...] = jnp.zeros_like(send_z)
-    loads[0].wait()
-    loads[1].wait()
-
-    def first(x, carry):
-        plane = pl.ds(x, 1)
-        pltpu.make_async_copy(f_hbm.at[:, plane], f_in.at[:, plane], load_sem.at[x]).wait()
-        collide_plane([f_in[q, x] for q in range(19)], x, 0)
-        return carry
-
-    lax.fori_loop(0, NX, first, 0, unroll=NX)
-    loads[NX + 2].wait()
-    loads[NX + 3].wait()
-
-    @pl.when(at_edge)
-    def _():
+    def make_filters():
         def component(a, carry):
             index = lax.broadcasted_iota(jnp.int32, (2 * NY, 4 * NY), 0)
             node = jnp.where(index < NY + 4, index, index - 2 * NY)
@@ -480,14 +494,73 @@
             reach_y = lax.broadcasted_iota(jnp.int32, (2 * NY, 4 * NY), 1) - NY - node
             reach_y = jnp.where(reach_y > 2 * NY - 1, reach_y - 4 * NY, reach_y)
             filter_y[a] = tap(reach_y, width[0, a]) * tap_norm(width[0, a])
-            index = lax.broadcasted_iota(jnp.int32, (3 * NZ, 2 * NZ), 1)
+            index = lax.broadcasted_iota(jnp.int32, (2 * NZ, 2 * NZ), 1)
             part = index & 3
             node = jnp.where(index < NZ, index, jnp.where(part < 2, part + NZ, part - 4))
-            reach_z = lax.broadcasted_iota(jnp.int32, (3 * NZ, 2 * NZ), 0) - NZ - node
+            index = lax.broadcasted_iota(jnp.int32, (2 * NZ, 2 * NZ), 0)
+            part = index - NZ
+            origin = jnp.where(part < 2 * REACH, part + NZ - REACH, 8 * NZ)
+            origin = jnp.where(part < REACH, part - REACH, origin)
+            reach_z = jnp.where(part < 0, index, origin) - node
             filter_z[a] = tap(reach_z, width[1, a]) * tap_norm(width[1, a])
             return carry
 
         lax.fori_loop(0, 3, component, 0)
+
+    def filter_steps(half):
+        await_rows(NOISE_ROWS[half], noise_recv.at[half])
+        outer = jnp.logical_or(row == 0, row == NY - 1)
+        for a in range(3):
+            across = []
+            for step in range(WIDE * half, WIDE * half + WIDE):
+                place = REACH * (3 * step + a)
+                blocks = []
+                for b in range(4):
+                    main = noise[b, step, a]
+                    sides = jnp.where(
+                        lane < REACH,
+                        spin(noise_side[b, 0], -place),
+                        spin(noise_side[b, 1], REACH - place),
+                    )
+                    if b == 3:
+                        main, sides = jnp.where(outer, main, 0.0), jnp.where(outer, sides, 0.0)
+                    blocks.append(jnp.concatenate([main, sides], 1))
+                across.append(
+                    jnp.dot(
+                        filter_y[a],
+                        jnp.concatenate(blocks, 0),
+                        precision=lax.Precision.HIGHEST,
+                        preferred_element_type=jnp.float32,
+                    )
+                )
+            turbulence[a] = jnp.dot(
+                jnp.concatenate(across, 0),
+                filter_z[a],
+                precision=lax.Precision.HIGHEST,
+                preferred_element_type=jnp.float32,
+            )
+        for k in range(WIDE):
+            rows = pl.ds(2 * NY * k, 2 * NY)
+            for q, value in enumerate(inflow([turbulence[a, rows] for a in range(3)])):
+                flow[k, q] = value
+
+    def inflow_at(step, q, form, packed):
+        return flow[step % WIDE, q, form * NY : (form + 1) * NY, packed * NZ : (packed + 1) * NZ]
+
+    send_z[...] = jnp.zeros_like(send_z)
+    loads[0].wait()
+    loads[1].wait()
+
+    def first(x, carry):
+        plane = pl.ds(x, 1)
+        pltpu.make_async_copy(f_hbm.at[:, plane], f_in.at[:, plane], load_sem.at[x]).wait()
+        collide_plane([f_in[q, x] for q in range(19)], x, 0)
+        return carry
+
+    lax.fori_loop(0, NX, first, 0, unroll=NX)
+    loads[NX + 2].wait()
+    loads[NX + 3].wait()
+    pl.when(at_edge)(pack_noise)
 
     expected = jnp.where(at_inlet, len(LEVEL) + len(UP), len(NEIGHBOURS))
     pl.semaphore_wait(barrier, expected + jnp.where(at_edge, len(BEYOND), 0))
@@ -503,21 +576,15 @@
         @pl.when(at_edge)
         def _():
             if half == 0:
-                for step in range(STEPS):
-                    for copy in noise_copies(step):
+                for part in range(HALVES):
+                    for copy in noise_copies(part):
                         copy.start()
-
-                @pl.when(at_inlet)
-                def _():
-                    pl.semaphore_wait(ready_sem, len(DOWN))
-                    for copy in face_copies(0, DOWN):
-                        copy.start()
-
-            for step in range(WIDE * half, WIDE * half + WIDE):
-                filter_step(step)
-
-        await_faces(half)
+                make_filters()
+            filter_steps(half)
+
+        await_faces(half, SHORT)
         unpack(half)
+        await_faces(half, LONG)
 
         step = WIDE * half
 
@@ -582,7 +649,7 @@
 
     @pl.when(at_edge)
     def _():
-        await_rows(STEPS * NOISE_ROWS, send_sem.at[1])
+        await_rows(sum(NOISE_ROWS), send_sem.at[1])
 
 
 def solution(mesh):
@@ -601,25 +668,27 @@
                 pltpu.VMEM((19, NX) + tile, jnp.float32),
                 pltpu.SMEM((15,), jnp.float32),
                 pltpu.VMEM((NX,) + tile, jnp.int32),
-                pltpu.VMEM((4, 3, STEPS, 3) + tile, jnp.float32),
+                pltpu.VMEM((4, STEPS, 3) + tile, jnp.float32),
+                pltpu.VMEM((2,) + tile, jnp.float32),
+                pltpu.VMEM((4, 2) + tile, jnp.float32),
                 pltpu.SMEM((2, 3), jnp.int32),
                 pltpu.VMEM((HALVES, PLANES, 20, 2) + tile, jnp.float32),
                 pltpu.VMEM((20, 2) + tile, jnp.float32),
                 pltpu.VMEM((PLANES - 2, 19, 2) + tile, jnp.float32),
                 pltpu.VMEM((19, 2) + tile, jnp.float32),
-                pltpu.VMEM((HALVES, PACKED) + tile, jnp.float32),
-                pltpu.VMEM((HALVES, 3, 2, 2, PACKED) + tile, jnp.float32),
+                pltpu.VMEM((HALVES, 2) + tile, jnp.float32),
+                pltpu.VMEM((HALVES, 3, 2, 2) + tile, jnp.float32),
                 pltpu.VMEM((3, 2 * NY, 4 * NY), jnp.float32),
-                pltpu.VMEM((3, 3 * NZ, 2 * NZ), jnp.float32),
-                pltpu.VMEM((STEPS, 3, 2 * NY, 2 * NZ), jnp.float32),
+                pltpu.VMEM((3, 2 * NZ, 2 * NZ), jnp.float32),
+                pltpu.VMEM((3, WIDE * 2 * NY, 2 * NZ), jnp.float32),
                 pltpu.VMEM((WIDE, 19, 2 * NY, 2 * NZ), jnp.float32),
                 pltpu.SemaphoreType.DMA((NX + 4,)),
                 pltpu.SemaphoreType.DMA((3,)),
+                pltpu.SemaphoreType.DMA((HALVES, 2)),
+                pltpu.SemaphoreType.DMA((HALVES, 2)),
                 pltpu.SemaphoreType.DMA((HALVES,)),
-                pltpu.SemaphoreType.DMA((HALVES,)),
-                pltpu.SemaphoreType.DMA((STEPS,)),
                 pltpu.SemaphoreType.REGULAR,
-                pltpu.VMEM((max(HALVES * OTHER_ROWS, STEPS * NOISE_ROWS), NZ), jnp.float32),
+                pltpu.VMEM((HALVES * OTHER_ROWS, NZ), jnp.float32),
             ],
             compiler_params=pltpu.CompilerParams(
                 collective_id=0, has_side_effects=True, vmem_limit_bytes=32 << 20

time: 29 us -> 24.2 us (0.83)
  Pallas kernels: 28.1 us -> 23.3 us
    pallas_call x1, Pallas kernels: 28.1 us -> 23.3 us  [local(): pl.pallas_call(functools.partial(kernel, counts), name='lattice_steps', o...]
where the time goes in v5:
time: 24.2 us; the launch traced here: 24 us
  Pallas kernels  23.3 us (96%)
  local copies, waits for them, and re-layouts  0.72 us (3%)
    pallas_call x1, Pallas kernels, local(): pl.pallas_call(functools.partial(kernel, counts), name='lattice_steps', o...  23.3 us
    unnamed x1, local copies, waits for them, and re-layouts  0.72 us

profile of v5, /device:TPU:1, one launch (start us, length us, event | category | flops | bytes accessed | tf_op | source)
XLA Modules:
  0.0 24.0 jit_solution(7045281698897799694)
XLA Ops:
  0.0 23.3 %lattice_steps.1 = f32[19,4,8,128]{3,2,1,0:T(8,128)S(1)} custom-call(f32[19,4,8,128]{3,2,1,0:T(8,128)} %f_hbm.1, f32[15]{0:T(128)} %rate_hbm.1, s32[4,8,128]{2,1,0:T(8,128)} %solid_hbm.1, f32[4,3,8,128]{3,2,1,0:T(8,128)} %noise_hbm.1, s32[2,3]{1,0:T(2,128)} %bitcast.1), custom_call_target="tpu_custom_call" | custom-call | tf_op jit(solution)/shard_map/lattice_steps/pallas_call | solution.py:661
  23.3 0.7 %copy.7 = f32[19,4,8,128]{3,2,1,0:T(8,128)} copy(f32[19,4,8,128]{3,2,1,0:T(8,128)S(1)} %lattice_steps.1) | data formatting | bytes 622592

commit v6 on v5

--- a/solution.py
+++ b/solution.py
@@ -49,6 +49,7 @@
     key=lambda d: -sum(map(abs, d)),
 )
 LEVEL, UP, DOWN = ([d for d in NEIGHBOURS if d[0] == step] for step in (0, 1, -1))
+STRAIGHT = (-1, 0, 0)
 ACROSS = [d for d in itertools.product((0,), (-1, 0, 1, 2), (-1, 0, 1)) if any(d)]
 BEYOND = [d for d in ACROSS if d[1] == 2]
 
@@ -104,6 +105,7 @@
 
 
 REACH = 10
+KNOWN_ROWS = 15 * NY
 NOISE_Y_ROWS = WIDE * 3 * (2 * NY + 2)
 NOISE_ROWS = [6 * NY + 2 * 2 + NOISE_Y_ROWS, NOISE_Y_ROWS]
 
@@ -300,12 +302,12 @@
         span = ruler.at[pl.ds(0, rows)]
         pltpu.make_async_copy(span, span, semaphore).wait()
 
-    def face_copies(half, offsets):
+    def face_copies(half, offsets, known=0):
         copies = []
         for offset in offsets:
             dx, dy, dz = offset
             form = 1 if dy else 0
-            for piece in pieces(offset):
+            for piece in pieces(offset)[known:]:
                 if dz:
                     rows = pl.ds(*piece)
                     source = send_z.at[half, 0 if dz > 0 else 1, rows]
@@ -362,30 +364,48 @@
         noise_z[0], noise_z[1] = above, below
 
     def send_faces(half):
-        @pl.when(jnp.logical_not(at_outlet))
-        def _():
-            for copy in face_copies(half, UP):
+        for kind in (SHORT, LONG):
+
+            @pl.when(jnp.logical_not(at_outlet))
+            def _():
+                for copy in face_copies(half, [d for d in UP if d in kind]):
+                    copy.start()
+
+            @pl.when(jnp.logical_not(at_inlet))
+            def _():
+                for copy in face_copies(half, [d for d in DOWN if d in kind]):
+                    copy.start()
+
+            for copy in face_copies(half, [d for d in LEVEL if d in kind]):
                 copy.start()
-
-        @pl.when(jnp.logical_not(at_inlet))
-        def _():
-            for copy in face_copies(half, DOWN):
-                copy.start()
-
-        for copy in face_copies(half, LEVEL):
-            copy.start()
         if half == 1:
 
             @pl.when(at_inlet)
             def _():
                 pl.semaphore_wait(ready_sem, len(DOWN))
                 for late in range(2):
-                    for copy in face_copies(late, DOWN):
+                    for kind in (SHORT, LONG):
+                        offsets = [d for d in DOWN if d in kind and d != STRAIGHT]
+                        for copy in face_copies(late, offsets):
+                            copy.start()
+                    for copy in face_copies(late, [STRAIGHT], late):
                         copy.start()
 
     def await_faces(half, kind):
         place = 0 if kind is SHORT else 1
-        await_rows(received(LEVEL + DOWN, kind), recv_sem.at[half, place])
+        rows = received(LEVEL + DOWN, kind)
+        if kind is LONG and half == 1:
+
+            @pl.when(at_outlet)
+            def _():
+                await_rows(rows - KNOWN_ROWS, recv_sem.at[half, place])
+
+            @pl.when(jnp.logical_not(at_outlet))
+            def _():
+                await_rows(rows, recv_sem.at[half, place])
+
+        else:
+            await_rows(rows, recv_sem.at[half, place])
 
         @pl.when(jnp.logical_not(at_inlet))
         def _():
@@ -547,6 +567,13 @@
     def inflow_at(step, q, form, packed):
         return flow[step % WIDE, q, form * NY : (form + 1) * NY, packed * NZ : (packed + 1) * NZ]
 
+    def collide_inlet():
+        blocked = post[0, WIDE + NX, PLACE[SOLID], 0]
+        result = collide([inflow_at(1, q, 0, 0) for q in range(19)], blocked > 0.5, rates())
+        for q, value in enumerate(result + [blocked]):
+            if PLACE[q] >= 5:
+                post[1, WIDE + NX, PLACE[q], 0] = value
+
     send_z[...] = jnp.zeros_like(send_z)
     loads[0].wait()
     loads[1].wait()
@@ -580,6 +607,8 @@
                     for copy in noise_copies(part):
                         copy.start()
                 make_filters()
+            else:
+                pl.when(at_outlet)(collide_inlet)
             filter_steps(half)
 
         await_faces(half, SHORT)
@@ -588,28 +617,32 @@
 
         step = WIDE * half
 
-        def around(index, carry):
-            plane = index + 1
+        def around(plane, edge=None):
+            index = plane - 1
             f = stream_plane(
                 plane,
                 lambda source, q, form: post[half, source, PLACE[q], form],
                 lambda q, form: side[PLACE[q], form],
                 True,
             )
-            set_here = jnp.logical_or(
-                jnp.logical_and(at_inlet, plane == WIDE),
-                jnp.logical_and(at_outlet, plane == WIDE + NX),
-            )
             for form in range(2):
-                f_form = [
-                    jnp.where(set_here, inflow_at(step, q, form, 0), f[form][q]) for q in range(19)
-                ]
+                f_form = f[form]
+                if edge is not None:
+                    f_form = [
+                        jnp.where(edge, inflow_at(step, q, form, 0), f_form[q]) for q in range(19)
+                    ]
                 result = collide(f_form, post[half, plane, PLACE[SOLID], form] > 0.5, rates())
                 for q in range(19):
                     later[index, q, form] = result[q]
+
+        def between(plane, carry):
+            around(plane)
             return carry
 
-        lax.fori_loop(0, PLANES - 2, around, 0, unroll=UNROLL)
+        around(1)
+        around(WIDE, at_inlet)
+        lax.fori_loop(WIDE + 1, WIDE + NX, between, 0, unroll=3)
+        around(WIDE + NX, at_outlet)
         f = stream_side(half)
         edge_plane = jnp.where(at_inlet, WIDE, WIDE + NX)
         set_here = jnp.logical_and(at_edge, (lane >> 2) == edge_plane)
@@ -641,7 +674,13 @@
 
         lax.fori_loop(0, NX, own, 0, unroll=NX)
 
-    await_rows(HALVES * OTHER_ROWS, send_sem.at[0])
+    @pl.when(at_inlet)
+    def _():
+        await_rows(HALVES * OTHER_ROWS - KNOWN_ROWS, send_sem.at[0])
+
+    @pl.when(jnp.logical_not(at_inlet))
+    def _():
+        await_rows(HALVES * OTHER_ROWS, send_sem.at[0])
 
     @pl.when(jnp.logical_not(at_outlet))
     def _():

time: 24.2 us -> 23.9 us (0.988)
  Pallas kernels: 23.3 us -> 23 us
    pallas_call x1, Pallas kernels: 23.3 us -> 23 us  [local(): pl.pallas_call(functools.partial(kernel, counts), name='lattice_steps', o...]
where the time goes in v6:
time: 23.9 us; the launch traced here: 23.7 us
  Pallas kernels  23 us (96%)
  local copies, waits for them, and re-layouts  0.72 us (3%)
    pallas_call x1, Pallas kernels, local(): pl.pallas_call(functools.partial(kernel, counts), name='lattice_steps', o...  23 us
    unnamed x1, local copies, waits for them, and re-layouts  0.72 us

profile of v6, /device:TPU:1, one launch (start us, length us, event | category | flops | bytes accessed | tf_op | source)
XLA Modules:
  0.0 23.7 jit_solution(18113525725534619017)
XLA Ops:
  0.0 23.0 %lattice_steps.1 = f32[19,4,8,128]{3,2,1,0:T(8,128)S(1)} custom-call(f32[19,4,8,128]{3,2,1,0:T(8,128)} %f_hbm.1, f32[15]{0:T(128)} %rate_hbm.1, s32[4,8,128]{2,1,0:T(8,128)} %solid_hbm.1, f32[4,3,8,128]{3,2,1,0:T(8,128)} %noise_hbm.1, s32[2,3]{1,0:T(2,128)} %bitcast.1), custom_call_target="tpu_custom_call" | custom-call | tf_op jit(solution)/shard_map/lattice_steps/pallas_call | solution.py:700
  23.0 0.7 %copy.7 = f32[19,4,8,128]{3,2,1,0:T(8,128)} copy(f32[19,4,8,128]{3,2,1,0:T(8,128)S(1)} %lattice_steps.1) | data formatting | bytes 622592

commit v7 on v6

--- a/solution.py
+++ b/solution.py
@@ -36,6 +36,7 @@
     (0, -1, 1),
 ]
 OPPOSITE = [0] + [q + 1 if q % 2 == 1 else q - 1 for q in range(1, 19)]
+NORMS = (2394.0, 12.0, 36.0, 4.0, 4.0, 4.0, 40.0, 40.0, 40.0, 8.0, 8.0, 8.0, 252.0, 24.0, 72.0)
 SOLID = 19
 ORDER = sorted(range(20), key=lambda q: (tuple(-c for c in (VELOCITY + [(0, 0, 0)])[q][:2]), q))
 PLACE = [ORDER.index(q) for q in range(20)]
@@ -136,27 +137,27 @@
     square = xx + yy + zz
     normal_xy, normal_z = xx - yy, 2.0 * zz - xx - yy
 
-    def relax(which, norm, value):
-        return (rate[which] * (1.0 / norm)) * value
+    def relax(which, value):
+        return rate[which] * value
 
     axis_xy, edge_xy = total[1] - total[3], p_xz - p_yz
     axis_z = 2.0 * total[5] - total[1] - total[3]
     edge_z = p_xz + p_yz - 2.0 * p_xy
-    m4 = relax(0, 2394.0, 8.0 * edge_sum - 11.0 * axis_sum - 30.0 * f[0] + 11.0 * rho - 19.0 * square)
-    m5 = relax(1, 12.0, axis_xy + edge_xy - normal_xy)
-    m6 = relax(2, 36.0, axis_z + edge_z - normal_z)
-    m7 = relax(3, 4.0, q_xy - j_x * u_y)
-    m8 = relax(4, 4.0, q_yz - j_y * u_z)
-    m9 = relax(5, 4.0, q_xz - j_x * u_z)
-    m10 = relax(6, 40.0, far_x - 4.0 * apart[1] + (2.0 / 3.0) * j_x)
-    m11 = relax(7, 40.0, far_y - 4.0 * apart[3] + (2.0 / 3.0) * j_y)
-    m12 = relax(8, 40.0, far_z - 4.0 * apart[5] + (2.0 / 3.0) * j_z)
-    m13 = relax(9, 8.0, a_xy - a_xz)
-    m14 = relax(10, 8.0, a_yz - b_xy)
-    m15 = relax(11, 8.0, b_xz - b_yz)
-    m16 = relax(12, 252.0, 12.0 * f[0] - 4.0 * axis_sum + edge_sum - 3.0 * rho + 5.5 * square)
-    m17 = relax(13, 24.0, edge_xy - 2.0 * axis_xy + 0.5 * normal_xy)
-    m18 = relax(14, 72.0, edge_z - 2.0 * axis_z + 0.5 * normal_z)
+    m4 = relax(0, 8.0 * edge_sum - 11.0 * axis_sum - 30.0 * f[0] + 11.0 * rho - 19.0 * square)
+    m5 = relax(1, axis_xy + edge_xy - normal_xy)
+    m6 = relax(2, axis_z + edge_z - normal_z)
+    m7 = relax(3, q_xy - j_x * u_y)
+    m8 = relax(4, q_yz - j_y * u_z)
+    m9 = relax(5, q_xz - j_x * u_z)
+    m10 = relax(6, far_x - 4.0 * apart[1] + (2.0 / 3.0) * j_x)
+    m11 = relax(7, far_y - 4.0 * apart[3] + (2.0 / 3.0) * j_y)
+    m12 = relax(8, far_z - 4.0 * apart[5] + (2.0 / 3.0) * j_z)
+    m13 = relax(9, a_xy - a_xz)
+    m14 = relax(10, a_yz - b_xy)
+    m15 = relax(11, b_xz - b_yz)
+    m16 = relax(12, 12.0 * f[0] - 4.0 * axis_sum + edge_sum - 3.0 * rho + 5.5 * square)
+    m17 = relax(13, edge_xy - 2.0 * axis_xy + 0.5 * normal_xy)
+    m18 = relax(14, edge_z - 2.0 * axis_z + 0.5 * normal_z)
 
     axis_base = -11.0 * m4 - 4.0 * m16
     edge_base = 8.0 * m4 + m16
@@ -233,6 +234,7 @@
     out,
     f_in,
     rate,
+    rate_tiles,
     solid,
     noise,
     noise_z,
@@ -412,7 +414,7 @@
             await_rows(received(UP, kind), recv_up.at[half, place])
 
     def rates():
-        return [rate[k] for k in range(15)]
+        return [rate_tiles[k] for k in range(15)]
 
     def collide_plane(f, x, half):
         blocked = solid[x] > 0
@@ -576,6 +578,8 @@
 
     send_z[...] = jnp.zeros_like(send_z)
     loads[0].wait()
+    for k in range(15):
+        rate_tiles[k] = jnp.full((NY, NZ), rate[k] * (1.0 / NORMS[k]), jnp.float32)
     loads[1].wait()
 
     def first(x, carry):
@@ -597,15 +601,19 @@
         for offset in UP:
             greet(offset, ready_sem)
 
+    @pl.when(at_edge)
+    def _():
+        for copy in noise_copies(0):
+            copy.start()
+
     for half in range(HALVES):
         send_faces(half)
 
         @pl.when(at_edge)
         def _():
             if half == 0:
-                for part in range(HALVES):
-                    for copy in noise_copies(part):
-                        copy.start()
+                for copy in noise_copies(1):
+                    copy.start()
                 make_filters()
             else:
                 pl.when(at_outlet)(collide_inlet)
@@ -706,6 +714,7 @@
             scratch_shapes=[
                 pltpu.VMEM((19, NX) + tile, jnp.float32),
                 pltpu.SMEM((15,), jnp.float32),
+                pltpu.VMEM((15,) + tile, jnp.float32),
                 pltpu.VMEM((NX,) + tile, jnp.int32),
                 pltpu.VMEM((4, STEPS, 3) + tile, jnp.float32),
                 pltpu.VMEM((2,) + tile, jnp.float32),

time: 23.9 us -> 23.2 us (0.971)
  Pallas kernels: 23 us -> 22.1 us
    pallas_call x1, Pallas kernels: 23 us -> 22.1 us  [local(): pl.pallas_call(functools.partial(kernel, counts), name='lattice_steps', o...]
where the time goes in v7:
time: 23.2 us; the launch traced here: 22.9 us
  Pallas kernels  22.1 us (95%)
  local copies, waits for them, and re-layouts  0.72 us (3%)
    pallas_call x1, Pallas kernels, local(): pl.pallas_call(functools.partial(kernel, counts), name='lattice_steps', o...  22.1 us
    unnamed x1, local copies, waits for them, and re-layouts  0.72 us

profile of v7, /device:TPU:1, one launch (start us, length us, event | category | flops | bytes accessed | tf_op | source)
XLA Modules:
  0.0 22.9 jit_solution(8103712568511454030)
XLA Ops:
  0.0 22.1 %lattice_steps.1 = f32[19,4,8,128]{3,2,1,0:T(8,128)S(1)} custom-call(f32[19,4,8,128]{3,2,1,0:T(8,128)} %f_hbm.1, f32[15]{0:T(128)} %rate_hbm.1, s32[4,8,128]{2,1,0:T(8,128)} %solid_hbm.1, f32[4,3,8,128]{3,2,1,0:T(8,128)} %noise_hbm.1, s32[2,3]{1,0:T(2,128)} %bitcast.1), custom_call_target="tpu_custom_call" | custom-call | tf_op jit(solution)/shard_map/lattice_steps/pallas_call | solution.py:708
  22.1 0.7 %copy.7 = f32[19,4,8,128]{3,2,1,0:T(8,128)} copy(f32[19,4,8,128]{3,2,1,0:T(8,128)S(1)} %lattice_steps.1) | data formatting | bytes 622592

commit v8 on v7

--- a/solution.py
+++ b/solution.py
@@ -324,7 +324,7 @@
                         src_ref=source,
                         dst_ref=target,
                         send_sem=send_sem.at[2 if dx > 0 else 0],
-                        recv_sem=(recv_up if dx > 0 else recv_sem).at[half, 0 if dz else 1],
+                        recv_sem=(recv_up if dx > 0 else recv_sem).at[half, 0 if dz else 2 if dx < 0 else 1],
                         device_id=neighbour(here, counts, offset),
                         device_id_type=MESH,
                     )
@@ -395,23 +395,26 @@
 
     def await_faces(half, kind):
         place = 0 if kind is SHORT else 1
-        rows = received(LEVEL + DOWN, kind)
-        if kind is LONG and half == 1:
-
-            @pl.when(at_outlet)
-            def _():
-                await_rows(rows - KNOWN_ROWS, recv_sem.at[half, place])
-
-            @pl.when(jnp.logical_not(at_outlet))
-            def _():
-                await_rows(rows, recv_sem.at[half, place])
-
-        else:
-            await_rows(rows, recv_sem.at[half, place])
+        offsets = LEVEL + DOWN if kind is SHORT else LEVEL
+        await_rows(received(offsets, kind), recv_sem.at[half, place])
 
         @pl.when(jnp.logical_not(at_inlet))
         def _():
             await_rows(received(UP, kind), recv_up.at[half, place])
+
+    def await_faces_from_above(half):
+        rows = received(DOWN, LONG)
+        if half == 0:
+            await_rows(rows, recv_sem.at[half, 2])
+        else:
+
+            @pl.when(at_outlet)
+            def _():
+                await_rows(rows - KNOWN_ROWS, recv_sem.at[half, 2])
+
+            @pl.when(jnp.logical_not(at_outlet))
+            def _():
+                await_rows(rows, recv_sem.at[half, 2])
 
     def rates():
         return [rate_tiles[k] for k in range(15)]
@@ -649,7 +652,9 @@
 
         around(1)
         around(WIDE, at_inlet)
-        lax.fori_loop(WIDE + 1, WIDE + NX, between, 0, unroll=3)
+        lax.fori_loop(WIDE + 1, WIDE + NX - 1, between, 0, unroll=2)
+        await_faces_from_above(half)
+        around(WIDE + NX - 1)
         around(WIDE + NX, at_outlet)
         f = stream_side(half)
         edge_plane = jnp.where(at_inlet, WIDE, WIDE + NX)
@@ -732,7 +737,7 @@
                 pltpu.VMEM((WIDE, 19, 2 * NY, 2 * NZ), jnp.float32),
                 pltpu.SemaphoreType.DMA((NX + 4,)),
                 pltpu.SemaphoreType.DMA((3,)),
-                pltpu.SemaphoreType.DMA((HALVES, 2)),
+                pltpu.SemaphoreType.DMA((HALVES, 3)),
                 pltpu.SemaphoreType.DMA((HALVES, 2)),
                 pltpu.SemaphoreType.DMA((HALVES,)),
                 pltpu.SemaphoreType.REGULAR,

time: 23.2 us -> 23.1 us (level)
  no operation moved by 1% of the time
where the time goes in v8:
time: 23.1 us; the launch traced here: 22.9 us
  Pallas kernels  22.2 us (96%)
  local copies, waits for them, and re-layouts  0.72 us (3%)
    pallas_call x1, Pallas kernels, local(): pl.pallas_call(functools.partial(kernel, counts), name='lattice_steps', o...  22.2 us
    unnamed x1, local copies, waits for them, and re-layouts  0.72 us

profile of v8, /device:TPU:1, one launch (start us, length us, event | category | flops | bytes accessed | tf_op | source)
XLA Modules:
  0.0 22.9 jit_solution(3845984846415872014)
XLA Ops:
  0.0 22.2 %lattice_steps.1 = f32[19,4,8,128]{3,2,1,0:T(8,128)S(1)} custom-call(f32[19,4,8,128]{3,2,1,0:T(8,128)} %f_hbm.1, f32[15]{0:T(128)} %rate_hbm.1, s32[4,8,128]{2,1,0:T(8,128)} %solid_hbm.1, f32[4,3,8,128]{3,2,1,0:T(8,128)} %noise_hbm.1, s32[2,3]{1,0:T(2,128)} %bitcast.1), custom_call_target="tpu_custom_call" | custom-call | tf_op jit(solution)/shard_map/lattice_steps/pallas_call | solution.py:713
  22.2 0.7 %copy.7 = f32[19,4,8,128]{3,2,1,0:T(8,128)} copy(f32[19,4,8,128]{3,2,1,0:T(8,128)S(1)} %lattice_steps.1) | data formatting | bytes 622592
